TPU v7x, 256 devices: a whole 4x4x8 slice. The times are simulated.
256 devices in a mesh: span: 16 (over z, core), normal: 16 (over x, y).
Axes of the slice: x: 4, y: 4, z: 8, core: 2. Of those that a mesh axis runs over, the one named last changes fastest.
Arguments:
- populations: float32 [19, 4, 256, 2048], P(None, None, 'normal', 'span'), as said below
- wall_mask: int32 [4, 256, 2048], P(None, 'normal', 'span'), may hold values from 0 to 1, as said below
- crop_anchors: int32 [16, 16, 12, 3], P('normal', 'span'), may hold values from 0 to 2032, as said below
- trainers: int32 [16, 16, 12, 1], P('normal', 'span'), may hold values from 0 to 15; in each aligned block of 12 rows (0 to 11, 12 to 23, ..., all dimensions but the last counted through in order) at most 2 rows name the same one
- w_lift: bfloat16 [16, 64, 108], P('span'), may hold values from -0.625 to 0.625
- b_lift: bfloat16 [16, 64], P('span'), may hold values from -1.75 to 1.75
- w_mix: bfloat16 [16, 64, 64], P('span'), may hold values from -0.75 to 0.75
- b_mix: bfloat16 [16, 64], P('span'), may hold values from -1.75 to 1.75
- w_head: bfloat16 [16, 4, 64], P('span'), may hold values from -0.75 to 0.75
- b_head: bfloat16 [16, 4], P('span'), may hold values from -1.75 to 1.75
Outputs:
- final_populations: float32 [19, 4, 256, 2048], P(None, None, 'normal', 'span')
- grad_w_lift: float32 [16, 64, 108], P('span')
- grad_b_lift: float32 [16, 64], P('span')
- grad_w_mix: float32 [16, 64, 64], P('span')
- grad_b_mix: float32 [16, 64], P('span')
- grad_w_head: float32 [16, 4, 64], P('span')
- grad_b_head: float32 [16, 4], P('span')
- member_loss: float32 [16], P('span')
Inputs may be any that keep to these rules, and one draw needn't show every extreme that they name: `populations`: every population is positive; density stays near 1 and flow speeds well below 0.3. `wall_mask`: 1 marks a solid cell; the first and the last wall-normal layer of cells are solid, and solid cells are scattered through the fluid. `crop_anchors`: entries are (along-flow, spanwise, wall-normal); a crop at row n of the first dimension and s of the second has along-flow anchor below 4, spanwise anchor at least s * 128 and at most (s + 1) * 128 - 16, wall-normal anchor at least n * 16 and at most (n + 1) * 16 - 16, so it lies inside that tile. `trainers`: among the 12 crops of one device no member is named more than 2 times, and in some device one member is named exactly 2 times.
All inputs are finite; a program needn't handle non-finite values.
Results may differ from a plain program's by a relative error of at most 0.0013.
Values may be sent and summed in bfloat16 or wider, within the bound.
A program may use at most 64 MiB of HBM per device.

v0:
```python
import functools

import jax
import jax.numpy as jnp
import numpy as np
from jax import lax
from jax.experimental import pallas as pl
from jax.experimental.pallas import tpu as pltpu
from jax.sharding import PartitionSpec as P

STEPS = 4
CROPS_DEV = 12
SX, CZ, CY = 4, 16, 128
EZ, EY = 24, 256
HID = 64
VOX = 512

VELOCITY = (
    (0, 0, 0),
    (1, 0, 0),
    (-1, 0, 0),
    (0, 1, 0),
    (0, -1, 0),
    (0, 0, 1),
    (0, 0, -1),
    (1, 1, 0),
    (-1, -1, 0),
    (1, -1, 0),
    (-1, 1, 0),
    (1, 0, 1),
    (-1, 0, -1),
    (1, 0, -1),
    (-1, 0, 1),
    (0, 1, 1),
    (0, -1, -1),
    (0, 1, -1),
    (0, -1, 1),
)
WEIGHTS = (1.0 / 3.0,) + (1.0 / 18.0,) * 6 + (1.0 / 36.0,) * 12
OPPOSITE = (0, 2, 1, 4, 3, 6, 5, 8, 7, 10, 9, 12, 11, 14, 13, 16, 15, 18, 17)
OMEGA = 1.25
SCALE_DENSITY = 50.0
SCALE_FLOW = 30.0
F32 = jnp.float32
BF16 = jnp.bfloat16
MESH = pl.DeviceIdType.MESH


def signed_sum(entries, factors):
    running = None
    for entry, factor in zip(entries, factors):
        if factor == 0:
            continue
        if running is None:
            running = entry if factor > 0 else -entry
        else:
            running = running + entry if factor > 0 else running - entry
    return running


def moments(states):
    density = states[0]
    for number in range(1, 19):
        density = density + states[number]
    inverse = 1.0 / density
    flows = []
    for axis_id in range(3):
        summed = signed_sum(states, [VELOCITY[number][axis_id] for number in range(19)])
        flows.append(summed * inverse)
    return (density, flows[0], flows[1], flows[2])


def collide(states, wet_cells):
    density, flow_x, flow_y, flow_z = moments(states)
    flows = (flow_x, flow_y, flow_z)
    speed_sq = flow_x * flow_x + flow_y * flow_y + flow_z * flow_z
    base = 1.0 - 1.5 * speed_sq
    result = [None] * 19
    kept = 1.0 - OMEGA
    scaled = {w: (OMEGA * w) * density for w in set(WEIGHTS)}
    relaxed = kept * states[0] + scaled[WEIGHTS[0]] * base
    result[0] = jnp.where(wet_cells, relaxed, states[0])
    for number in range(1, 19, 2):
        other = OPPOSITE[number]
        along = signed_sum(flows, VELOCITY[number])
        weight = scaled[WEIGHTS[number]]
        even = weight * (base + (4.5 * along) * along)
        odd = weight * (3.0 * along)
        forth = kept * states[number] + (even + odd)
        back = kept * states[other] + (even - odd)
        result[number] = jnp.where(wet_cells, forth, states[other])
        result[other] = jnp.where(wet_cells, back, states[number])
    return result


def features(states, fluid):
    density, flow_x, flow_y, flow_z = moments(states)
    return [
        (density - 1.0) * SCALE_DENSITY * fluid,
        flow_x * SCALE_FLOW * fluid,
        flow_y * SCALE_FLOW * fluid,
        flow_z * SCALE_FLOW * fluid,
    ]


def lattice_kernel(
    ns,
    nn,
    pop,
    wall,
    wb,
    fin,
    feat,
    wall_w,
    pack_l,
    pack_r,
    pack_u,
    pack_d,
    got_l,
    got_r,
    got_u,
    got_d,
    got_c,
    weights,
    cells,
    post,
    halo_send,
    halo_recv,
    ag_send,
    ag_recv,
    fw_send,
    fw_recv,
):
    s = lax.axis_index("span")
    n = lax.axis_index("normal")
    chips = ns // 2
    chip = s // 2
    core = s % 2
    right, left = (s + 1) % ns, (s + ns - 1) % ns
    up, down = (n + 1) % nn, (n + nn - 1) % nn
    sibling = chip * 2 + (1 - core)

    def place(nn_, ss_):
        return {"normal": nn_, "span": ss_}

    peers = [
        place(n, right),
        place(n, left),
        place(up, s),
        place(down, s),
        place(up, right),
        place(up, left),
        place(down, right),
        place(down, left),
        place(n, sibling),
    ]
    z_peers = [((chip + k) % chips) * 2 + core for k in range(1, chips)]
    peers += [place(n, peer) for peer in z_peers]
    barrier = pltpu.get_barrier_semaphore()
    for peer in peers:
        pl.semaphore_signal(barrier, inc=1, device_id=peer, device_id_type=MESH)

    sub = lax.broadcasted_iota(jnp.int32, (8, 128), 0)
    low = sub < 4

    def field_of(k):
        return pop[k] if k < 19 else wall[...].astype(F32)

    for k in range(20):
        f = field_of(k)
        for j in range(2):
            t0, t1 = f[2 * j], f[2 * j + 1]
            pack_u[k, j] = jnp.where(low, pltpu.roll(t1[8:16], 4, 0), t0[8:16])
            pack_d[k, j] = jnp.where(low, t0[0:8], pltpu.roll(t1[0:8], 4, 0))
    pl.semaphore_wait(barrier, len(peers))

    def halo(i, src, dst, peer):
        return pltpu.make_async_remote_copy(
            src_ref=src,
            dst_ref=dst,
            send_sem=halo_send.at[i],
            recv_sem=halo_recv.at[i],
            device_id=peer,
            device_id_type=MESH,
        )

    sends = [
        halo(0, pack_u, got_u, place(up, s)),
        halo(1, pack_d, got_d, place(down, s)),
    ]
    for copy in sends:
        copy.start()

    slot = lax.broadcasted_iota(jnp.int32, (64, 128), 1) // 4
    pl_val = jnp.ones((64, 128), F32)
    pr_val = jnp.ones((64, 128), F32)
    for k in range(20):
        f = field_of(k).reshape(64, 128)
        rolled = pltpu.roll(f, 4 * k, 1) if k else f
        pl_val = jnp.where(slot == k, rolled, pl_val)
        pr_val = jnp.where(slot == (k - 1) % 32, rolled, pr_val)
    pack_l[...] = pl_val.reshape(SX, CZ, CY)
    pack_r[...] = pr_val.reshape(SX, CZ, CY)
    top, bottom = pl.ds(8, 8), pl.ds(0, 8)
    more = [
        halo(2, pack_l, got_l, place(n, left)),
        halo(3, pack_r, got_r, place(n, right)),
        halo(4, pack_l.at[:, bottom, :], got_c.at[0], place(down, left)),
        halo(5, pack_l.at[:, top, :], got_c.at[1], place(up, left)),
        halo(6, pack_r.at[:, bottom, :], got_c.at[2], place(down, right)),
        halo(7, pack_r.at[:, top, :], got_c.at[3], place(up, right)),
    ]
    for copy in more:
        copy.start()
    sends += more

    gathers = []
    for k, peer in enumerate(z_peers):
        gathers.append(
            pltpu.make_async_remote_copy(
                src_ref=wb,
                dst_ref=weights.at[s],
                send_sem=ag_send.at[k],
                recv_sem=ag_recv.at[k],
                device_id=place(n, peer),
                device_id_type=MESH,
            )
        )
    for copy in gathers:
        copy.start()

    def forward(i, src, owner):
        return pltpu.make_async_remote_copy(
            src_ref=src,
            dst_ref=weights.at[owner],
            send_sem=fw_send.at[i],
            recv_sem=fw_recv.at[i],
            device_id=place(n, sibling),
            device_id_type=MESH,
        )

    forwards = [forward(0, wb, s)]
    forwards[0].start()
    wall_w[s] = wb[...]

    for k in range(20):
        cells[k, :, 0:CZ, 0:CY] = field_of(k)
    fluid = (1 - wall[...]).astype(F32)
    before = features([pop[k] for k in range(19)], fluid)

    for copy in sends:
        copy.wait()

    low4 = jnp.broadcast_to(low[None], (SX, 8, 128))
    edge_l = jnp.concatenate([got_l[...], jnp.where(low4, got_c[0], got_c[1])], axis=1)
    edge_r = jnp.concatenate([got_r[...], jnp.where(low4, got_c[2], got_c[3])], axis=1)
    edge_l = edge_l.reshape(SX * EZ, 128)
    edge_r = edge_r.reshape(SX * EZ, 128)
    odd = (lax.broadcasted_iota(jnp.int32, (SX * EZ, 128), 1) // 4) % 2 == 1
    mixed = (jnp.where(odd, edge_r, edge_l), jnp.where(odd, edge_l, edge_r))
    for k in range(20):
        side = mixed[k % 2]
        if k:
            side = pltpu.roll(side, 128 - 4 * k, 1)
        cells[k, :, :, CY:EY] = side.reshape(SX, EZ, 128)
        for j in range(2):
            u, d = got_u[k, j], got_d[k, j]
            cells[k, 2 * j, CZ:EZ, 0:CY] = jnp.where(low, d, u)
            cells[k, 2 * j + 1, CZ:EZ, 0:CY] = pltpu.roll(jnp.where(low, u, d), 4, 0)

    def one_step(step, carry):
        def one_chunk(i, inner):
            x = i // 3
            rows = pl.ds(pl.multiple_of((i % 3) * 8, 8), 8)
            states = [cells[q, x, rows, :] for q in range(19)]
            wet = cells[19, x, rows, :] < 0.5
            for q, value in enumerate(collide(states, wet)):
                post[q, x, rows, :] = value
            return inner

        lax.fori_loop(0, 12, one_chunk, 0)

        def one_slab(x, inner):
            for q in range(19):
                cx, cy, cz = VELOCITY[q]
                slab = post[q, (x + SX - cx) % SX]
                if cz:
                    slab = pltpu.roll(slab, cz % EZ, 0)
                if cy:
                    slab = pltpu.roll(slab, cy % EY, 1)
                cells[q, x] = slab
            return inner

        lax.fori_loop(0, SX, one_slab, 0)
        return carry

    lax.fori_loop(0, 2, one_step, 0)
    for k in range(1, chips):
        gathers[k - 1].wait()
        owner = ((chip + chips - k) % chips) * 2 + core
        copy = forward(k, weights.at[owner], owner)
        copy.start()
        forwards.append(copy)
        wall_w[owner] = weights[owner]
    lax.fori_loop(2, STEPS, one_step, 0)

    final = [cells[q, :, 0:CZ, 0:CY] for q in range(19)]
    for q in range(19):
        fin[q] = final[q]
    after = features(final, fluid)
    for c in range(4):
        feat[:, c] = before[c].astype(BF16)
        feat[:, 4 + c] = (after[c] - before[c]).astype(BF16)
    feat[:, 8] = fluid.astype(BF16)
    for copy in forwards:
        copy.wait()
    for k in range(chips):
        owner = ((chip + chips - k) % chips) * 2 + (1 - core)
        wall_w[owner] = weights[owner]


def gelu_both(x):
    c1, c2 = 0.7978845608028654, 0.7978845608028654 * 0.044715
    sq = x * x
    half = 0.5 * jnp.tanh(x * (c1 + c2 * sq)) + 0.5
    value = x * half
    slope = half + value * (1.0 - half) * (2.0 * c1 + 6.0 * c2 * sq)
    return value, slope


NT = (((1,), (1,)), ((), ()))
TN = (((0,), (0,)), ((), ()))


def dot(a, b, dims=(((1,), (0,)), ((), ()))):
    return lax.dot_general(a, b, dims, preferred_element_type=F32)


SHIFTS = [(a, b, c) for a in (-1, 0, 1) for b in (-1, 0, 1) for c in (-1, 0, 1)]


def constants():
    row = np.arange(288)
    lane = np.arange(256)
    spread = (lane[None, :] // 16 == row[:, None] % 16).astype(np.float32)
    select = np.zeros((48, 576), np.float32)
    for kind in range(3):
        for xi in range(2):
            for i in range(8):
                crop, channel = i // 4, i % 4
                f = (channel, 4 + channel, 8)[kind]
                start = crop * 288 + xi * 144 + f * 16
                select[kind * 16 + xi * 8 + i, start : start + 16] = 1.0
    expand = np.zeros((2, 128, 256), np.float32)
    for pos in range(2):
        for k in range(27):
            for c in range(4):
                expand[pos, 4 * k + c, 8 * k + 4 * pos + c] = 1.0
        expand[pos, 108, 216] = 1.0
    voxel = np.arange(VOX)
    vx, vz, vy = voxel // 256, voxel // 16 % 16, voxel % 16
    inside = np.ones((256, VOX), np.float32)
    for k, (dx, dz, dy) in enumerate(SHIFTS):
        good = (
            (vx + dx >= 0)
            & (vx + dx < 2)
            & (vz + dz >= 0)
            & (vz + dz < 16)
            & (vy + dy >= 0)
            & (vy + dy < 16)
        )
        inside[8 * k : 8 * k + 8] = good[None]
    return (
        jnp.asarray(spread),
        jnp.asarray(select, BF16),
        jnp.asarray(expand, BF16),
        jnp.asarray(np.transpose(expand, (0, 2, 1)), BF16),
        jnp.asarray(inside, BF16),
    )


def train_kernel(
    anchors, trainers, feat, wall_w, spread, select, expand, shrink, inside, grads
):
    def clear(i, carry):
        grads[i % 2, i // 2] = jnp.zeros((128, 128), F32)
        return carry

    lax.fori_loop(0, grads.shape[0] * grads.shape[1], clear, 0)
    unit_row = (lax.broadcasted_iota(jnp.int32, (64, VOX), 0) == 0).astype(F32)
    unit = unit_row.astype(BF16)
    lane64 = lax.broadcasted_iota(jnp.int32, (64, 128), 1)
    lane128 = lax.broadcasted_iota(jnp.int32, (128, 128), 1)
    pick_row = lax.broadcasted_iota(jnp.int32, (128, 256), 0)
    pick_lane = lax.broadcasted_iota(jnp.int32, (128, 256), 1) % 16
    ahead = pick_row - pick_lane

    def one_pair(i, carry):
        parts, owners = [], []
        for j in range(2):
            crop = 2 * i + j
            ox = anchors[0, 0, crop, 0]
            oy = anchors[0, 0, crop, 1] % CY
            owners.append(trainers[0, 0, crop, 0])
            near = feat[ox].reshape(144, 128)
            far = feat[(ox + 1) % SX].reshape(144, 128)
            window = (ahead == oy).astype(F32).astype(BF16)
            wide = dot(jnp.concatenate([near, far], axis=0), window)
            parts.append((wide * spread[...]).astype(BF16))
        rows = dot(select[...], jnp.concatenate(parts, axis=0))
        x8 = jnp.concatenate([rows[0:8], rows[8:16]], axis=1)
        t8 = jnp.concatenate([rows[16:24], rows[24:32]], axis=1)
        w8 = jnp.concatenate([rows[32:40], rows[40:48]], axis=1)
        moved = []
        for dx, dz, dy in SHIFTS:
            shift = (-(dx * 256 + dz * 16 + dy)) % VOX
            moved.append(pltpu.roll(x8, shift, 1) if shift else x8)
        moved.append(unit_row[0:40])
        patches = jnp.concatenate(moved, axis=0).astype(BF16) * inside[...]
        mats = [wall_w[owner] for owner in owners]
        lift = jnp.concatenate(
            [dot(mats[j][0:64], expand[j]) for j in range(2)], axis=0
        ).astype(BF16)
        h1f, slope1 = gelu_both(dot(lift, patches))
        h1 = h1f.astype(BF16)
        slopes2, h1s, h2s, pred = [], [], [], None
        for j in range(2):
            own = h1[64 * j : 64 * j + 64]
            ext = jnp.concatenate([own, unit], axis=0)
            z2 = dot(mats[j][64:128], ext)
            g2, slope2 = gelu_both(z2)
            h2 = (own.astype(F32) + g2).astype(BF16)
            ext2 = jnp.concatenate([h2, unit], axis=0)
            out = dot(mats[j][128:144], ext2)[8 * j : 8 * j + 8]
            pred = out if pred is None else pred + out
            slopes2.append(slope2)
            h1s.append(ext)
            h2s.append(ext2)
        missed = pred - t8
        weighted = w8 * missed
        loss8 = weighted * missed * (1.0 / (4.0 * VOX))
        dpred = weighted * (2.0 / (4.0 * VOX))
        errors = jnp.concatenate([dpred, loss8], axis=0).astype(BF16)
        errors = jnp.concatenate([jnp.zeros((112, VOX), BF16), errors], axis=0)
        dh1s, firsts = [], []
        for j in range(2):
            low = 112 + 4 * j
            keep = (lane64 >= low) & (lane64 < low + 4)
            head = jnp.where(keep, mats[j][0:64].astype(F32), 0.0).astype(BF16)
            dh2 = dot(head, errors)
            dz2 = (dh2 * slopes2[j]).astype(BF16)
            back = dot(mats[j][64:128, 0:64], dz2, TN)
            dh1s.append(dh2 + back)
            mixed = dot(dz2, h1s[j], NT)
            heads = dot(h2s[j], errors, NT)
            mine = (lane128 // 4) % 2 == j
            firsts.append((mixed, jnp.where(mine, heads, 0.0)))
        dz1 = (jnp.concatenate(dh1s, axis=0) * slope1).astype(BF16)
        lifted = dot(dz1, patches, NT).astype(BF16)
        for j in range(2):
            mixed, heads = firsts[j]
            small = dot(lifted[64 * j : 64 * j + 64], shrink[j])
            upper = (small + heads[0:64]).astype(BF16).astype(F32)
            lower = mixed + heads[64:128]
            lower = jnp.where(lane64 < 64, lower.astype(BF16).astype(F32), lower)
            owner = owners[j]
            both = jnp.concatenate([upper, lower], axis=0)
            grads[owner % 2, owner // 2] = grads[owner % 2, owner // 2] + both
        return carry

    lax.fori_loop(0, CROPS_DEV // 2, one_pair, 0)


def reduce_kernel(
    ns,
    nn,
    grads,
    out,
    pair,
    held,
    parts,
    zparts,
    mine,
    whole,
    pair_send,
    pair_recv,
    rs_send,
    rs_recv,
    z_send,
    z_recv,
    ag_send,
    ag_recv,
):
    s = lax.axis_index("span")
    n = lax.axis_index("normal")
    chips = ns // 2
    chip = s // 2
    core = s % 2
    sibling = chip * 2 + (1 - core)
    rows = 128 // nn
    n_peers = [(n + k) % nn for k in range(1, nn)]
    z_peers = [(chip + k) % chips for k in range(1, chips)]
    barrier = pltpu.get_barrier_semaphore()

    def at_span(other):
        return {"span": other, "normal": n}

    def at_normal(other):
        return {"span": s, "normal": other}

    peers = [at_span(sibling)]
    peers += [at_normal(other) for other in n_peers]
    peers += [at_span(other * 2 + core) for other in z_peers]
    for peer in peers:
        pl.semaphore_signal(barrier, inc=1, device_id=peer, device_id_type=MESH)
    pl.semaphore_wait(barrier, len(peers))

    def remote(src, dst, send, recv, peer):
        copy = pltpu.make_async_remote_copy(
            src_ref=src,
            dst_ref=dst,
            send_sem=send,
            recv_sem=recv,
            device_id=peer,
            device_id_type=MESH,
        )
        copy.start()
        return copy

    first = remote(
        grads.at[1 - core], pair, pair_send.at[0], pair_recv.at[0], at_span(sibling)
    )
    first.wait()
    for z in range(chips):
        held[z] = grads[core, z] + pair[z]
    seconds = []
    for k, other in enumerate(n_peers):
        chunk = pl.ds(pl.multiple_of(other * rows, 8), rows)
        seconds.append(
            remote(
                held.at[:, chunk, :],
                parts.at[k],
                rs_send.at[k],
                rs_recv.at[k],
                at_normal(other),
            )
        )
    own = held[:, pl.ds(pl.multiple_of(n * rows, 8), rows), :]
    for k in range(nn - 1):
        seconds[k].wait()
        own = own + parts[k]
    mine[...] = own
    thirds = []
    for k, other in enumerate(z_peers):
        thirds.append(
            remote(
                mine.at[other],
                zparts.at[k],
                z_send.at[k],
                z_recv.at[k],
                at_span(other * 2 + core),
            )
        )
    total = mine[chip]
    for k in range(chips - 1):
        thirds[k].wait()
        total = total + zparts[k]
    whole[n] = total * (1.0 / (CROPS_DEV * nn))
    fourths = []
    for k, other in enumerate(n_peers):
        fourths.append(
            remote(
                whole.at[n], whole.at[n], ag_send.at[k], ag_recv.at[k], at_normal(other)
            )
        )
    for copy in fourths:
        copy.wait()
    out[...] = whole[...]


def local(
    populations, wall_mask, crop_anchors, trainers, w_lift, b_lift, w_mix, b_mix, w_head, b_head
):
    ns, nn = lax.axis_size("span"), lax.axis_size("normal")
    chips = ns // 2
    vmem = pl.BlockSpec(memory_space=pltpu.VMEM)
    smem = pl.BlockSpec(memory_space=pltpu.SMEM)
    dma = pltpu.SemaphoreType.DMA
    turned = w_head[0].T
    zeros = functools.partial(jnp.zeros, dtype=BF16)
    heads = jnp.concatenate([w_head[0], b_head[0][:, None], zeros((4, 63))], axis=1)
    wb = jnp.concatenate(
        [
            jnp.concatenate(
                [w_lift[0], b_lift[0][:, None], zeros((64, 3)), turned, turned, zeros((64, 8))],
                axis=1,
            ),
            jnp.concatenate([w_mix[0], b_mix[0][:, None], zeros((64, 63))], axis=1),
            heads,
            zeros((8, 128)),
            heads,
        ],
        axis=0,
    )
    final, feat, wall_w = pl.pallas_call(
        functools.partial(lattice_kernel, ns, nn),
        out_shape=(
            jax.ShapeDtypeStruct((19, SX, CZ, CY), F32),
            jax.ShapeDtypeStruct((SX, 9, CZ, CY), BF16),
            jax.ShapeDtypeStruct((ns, 144, 128), BF16),
        ),
        in_specs=[vmem] * 3,
        out_specs=(vmem,) * 3,
        scratch_shapes=[
            pltpu.VMEM((SX, CZ, CY), F32),
            pltpu.VMEM((SX, CZ, CY), F32),
            pltpu.VMEM((20, 2, 8, 128), F32),
            pltpu.VMEM((20, 2, 8, 128), F32),
            pltpu.VMEM((SX, CZ, CY), F32),
            pltpu.VMEM((SX, CZ, CY), F32),
            pltpu.VMEM((20, 2, 8, 128), F32),
            pltpu.VMEM((20, 2, 8, 128), F32),
            pltpu.VMEM((4, SX, 8, 128), F32),
            pltpu.VMEM((ns, 144, 128), BF16),
            pltpu.VMEM((20, SX, EZ, EY), F32),
            pltpu.VMEM((19, SX, EZ, EY), F32),
            dma((8,)),
            dma((8,)),
            dma((chips,)),
            dma((chips,)),
            dma((chips,)),
            dma((chips,)),
        ],
        compiler_params=pltpu.CompilerParams(
            collective_id=0, has_side_effects=True, vmem_limit_bytes=48 << 20
        ),
        name="lattice",
    )(populations, wall_mask, wb)

    grads = pl.pallas_call(
        train_kernel,
        out_shape=jax.ShapeDtypeStruct((2, chips, 128, 128), F32),
        in_specs=[smem, smem] + [vmem] * 7,
        out_specs=vmem,
        compiler_params=pltpu.CompilerParams(vmem_limit_bytes=48 << 20),
        name="train",
    )(crop_anchors, trainers, feat, wall_w, *constants())

    rows = 128 // nn
    total = pl.pallas_call(
        functools.partial(reduce_kernel, ns, nn),
        out_shape=jax.ShapeDtypeStruct((nn, rows, 128), F32),
        in_specs=[vmem],
        out_specs=vmem,
        scratch_shapes=[
            pltpu.VMEM((chips, 128, 128), F32),
            pltpu.VMEM((chips, 128, 128), F32),
            pltpu.VMEM((nn - 1, chips, rows, 128), F32),
            pltpu.VMEM((chips - 1, rows, 128), F32),
            pltpu.VMEM((chips, rows, 128), F32),
            pltpu.VMEM((nn, rows, 128), F32),
            dma((1,)),
            dma((1,)),
            dma((nn - 1,)),
            dma((nn - 1,)),
            dma((chips - 1,)),
            dma((chips - 1,)),
            dma((nn - 1,)),
            dma((nn - 1,)),
        ],
        compiler_params=pltpu.CompilerParams(
            collective_id=1, has_side_effects=True, vmem_limit_bytes=48 << 20
        ),
        name="reduce",
    )(grads)
    total = total.reshape(128, 128)
    heads = total[:65, 112:116] + total[:65, 116:120]
    return (
        final,
        total[None, :64, :108],
        total[None, :64, 108],
        total[None, 64:, :64],
        total[None, 64:, 64],
        heads[:64].T[None],
        heads[64][None],
        jnp.sum(total[64, 120:128])[None],
    )


def solution(mesh):
    return jax.shard_map(
        local,
        mesh=mesh,
        in_specs=(
            P(None, None, "normal", "span"),
            P(None, "normal", "span"),
            P("normal", "span", None, None),
            P("normal", "span", None, None),
            P("span", None, None),
            P("span", None),
            P("span", None, None),
            P("span", None),
            P("span", None, None),
            P("span", None),
        ),
        out_specs=(
            P(None, None, "normal", "span"),
            P("span", None, None),
            P("span", None),
            P("span", None, None),
            P("span", None),
            P("span", None, None),
            P("span", None),
            P("span"),
        ),
        check_vma=False,
    )
```

profile of v0, /device:TPU:8, one launch (start us, length us, event | category | flops | bytes accessed | tf_op | source)
XLA Modules:
  0.0 73.3 jit_solution(6642239482374049581)
XLA Ops:
  0.7 0.6 copy-done.14
  1.3 0.1 copy.34
  1.4 0.6 copy-done.9
  2.1 0.6 copy-done.10
  2.8 0.6 copy-done.11
  3.4 0.6 copy-done.12
  4.0 0.1 copy.30
  4.1 0.5 copy-done.13
  4.6 0.1 copy.33
  4.8 0.1 copy.31
  5.0 0.7 copy-done.8
  5.7 0.1 concatenate.12
  5.8 0.1 concatenate.15.wb
  5.9 1.1 %copy-done = f32[19,4,16,128]{3,2,1,0:T(8,128)S(1)} copy-done((f32[19,4,16,128]{3,2,1,0:T(8,128)S(1)}, f32[19,4,16,128]{3,2,1,0:T(8,128)}, u32[]{:S(2)}) %copy-start) | copy-done | bytes 622616
  7.0 21.0 %lattice.1 = (f32[19,4,16,128]{3,2,1,0:T(8,128)S(1)}, bf16[4,9,16,128]{3,2,1,0:T(8,128)(2,1)S(1)}, bf16[16,144,128]{2,1,0:T(8,128)(2,1)S(1)}) custom-call(f32[19,4,16,128]{3,2,1,0:T(8,128)S(1)} %copy-done, s32[4,16,128]{2,1,0:T(8,128)S(1)} %copy-done.6, bf16[144,128]{1,0:T(8,128)(2,1)S(1)} %concatenate.15.wb), custom_call_target="tpu_custom_call" | custom-call | tf_op jit(solution)/shard_map/lattice/pallas_call | solution.py:605
  28.1 12.6 %train.1.grads = f32[2,8,128,128]{3,2,1,0:T(8,128)S(1)} custom-call(s32[1,1,12,3]{3,2,1,0:T(8,128)S(1)} %copy.35.anchors, s32[1,1,12,1]{3,2,1,0:T(8,128)S(1)} %copy.36.trainers, bf16[4,9,16,128]{3,2,1,0:T(8,128)(2,1)S(1)} %get-tuple-element.12.feat, bf16[16,144,128]{2,1,0:T(8,128)(2,1)S(1)} %get-tuple-element.13.wall_w, f32[288,256]{1,0:T(8,128)S(1)} %copy-done.1, ...), custom_call_target="tpu_custom_call" | custom-call | tf_op jit(solution)/shard_map/train/pallas_call | solution.py:640
  40.8 27.9 %reduce.6 = f32[16,8,128]{2,1,0:T(8,128)S(1)} custom-call(f32[2,8,128,128]{3,2,1,0:T(8,128)S(1)} %train.1.grads), custom_call_target="tpu_custom_call" | custom-call | tf_op jit(solution)/shard_map/reduce/pallas_call | solution.py:650
  68.7 0.7 slice_reduce_fusion.2
  69.3 0.7 slice_reduce_fusion
  70.0 0.6 slice_bitcast_fusion.1
  70.6 0.6 slice_bitcast_fusion.2
  71.3 0.5 slice.43
  71.9 0.7 copy.37
  72.5 0.8 %copy.39 = f32[19,4,16,128]{3,2,1,0:T(8,128)} copy(f32[19,4,16,128]{3,2,1,0:T(8,128)S(1)} %get-tuple-element.24) | data formatting | bytes 1245184
  (33 shorter events, 0.6 us)
Async XLA Ops:
  0.6 0.7 copy-start.14
  1.3 0.7 copy-start.9
  2.0 0.7 copy-start.10
  2.7 0.7 copy-start.11
  3.3 0.7 copy-start.12
  4.0 0.7 copy-start.13
  4.0 0.8 %copy-start.7 = (bf16[1,64,64]{2,1,0:T(8,128)(2,1)S(1)}, bf16[1,64,64]{2,1,0:T(8,128)(2,1)}, u32[]{:S(2)}) copy-start(bf16[1,64,64]{2,1,0:T(8,128)(2,1)} %param.21) | copy-start | bytes 24580
  4.8 1.1 %copy-start.6 = (s32[4,16,128]{2,1,0:T(8,128)S(1)}, s32[4,16,128]{2,1,0:T(8,128)}, u32[]{:S(2)}) copy-start(s32[4,16,128]{2,1,0:T(8,128)} %wall.1) | copy-start | bytes 98308
  4.9 0.7 copy-start.8
  5.0 23.1 %copy-start.5 = (bf16[48,576]{1,0:T(8,128)(2,1)S(1)}, bf16[48,576]{1,0:T(8,128)(2,1)}, u32[]{:S(2)}) copy-start(bf16[48,576]{1,0:T(8,128)(2,1)} %constant.10.clone.select) | copy-start | bytes 165892
  5.7 22.4 %copy-start.4 = (bf16[2,128,256]{2,1,0:T(8,128)(2,1)S(1)}, bf16[2,128,256]{2,1,0:T(8,128)(2,1)}, u32[]{:S(2)}) copy-start(bf16[2,128,256]{2,1,0:T(8,128)(2,1)} %constant.5.clone.expand) | copy-start | bytes 393220
  5.9 1.1 %copy-start = (f32[19,4,16,128]{3,2,1,0:T(8,128)S(1)}, f32[19,4,16,128]{3,2,1,0:T(8,128)}, u32[]{:S(2)}) copy-start(f32[19,4,16,128]{3,2,1,0:T(8,128)} %pop.1) | copy-start | bytes 1867780
  7.0 21.1 %copy-start.1 = (f32[288,256]{1,0:T(8,128)S(1)}, f32[288,256]{1,0:T(8,128)}, u32[]{:S(2)}) copy-start(f32[288,256]{1,0:T(8,128)} %constant.9.clone.spread) | copy-start | bytes 884740
  7.0 21.1 %copy-start.2 = (bf16[256,512]{1,0:T(8,128)(2,1)S(1)}, bf16[256,512]{1,0:T(8,128)(2,1)}, u32[]{:S(2)}) copy-start(bf16[256,512]{1,0:T(8,128)(2,1)} %constant.22.clone.inside) | copy-start | bytes 786436
  7.0 21.1 %copy-start.3 = (bf16[2,256,128]{2,1,0:T(8,128)(2,1)S(1)}, bf16[2,256,128]{2,1,0:T(8,128)(2,1)}, u32[]{:S(2)}) copy-start(bf16[2,256,128]{2,1,0:T(8,128)(2,1)} %constant.6.clone.shrink) | copy-start | bytes 393220
where the time goes:
time: 73.6 us; the launch traced here: 73.3 us
  Pallas kernels  61.6 us (84%)
  local copies, waits for them, and re-layouts  10.1 us (14%)
  other arithmetic  0.91 us (1%)
  between operations  0.78 us (1%)
    pallas_call x1, Pallas kernels, local(): pl.pallas_call(functools.partial(reduce_kernel, ns, nn), out_shape=jax.Sh...  27.9 us
    pallas_call x1, Pallas kernels, local(): pl.pallas_call(functools.partial(lattice_kernel, ns, nn), out_shape=(jax....  21 us
    pallas_call x1, Pallas kernels, local(): pl.pallas_call(train_kernel, out_shape=jax.ShapeDtypeStruct((2, chips, 12...  12.6 us
    unnamed x33, local copies, waits for them, and re-layouts  6.21 us

commit v1 on v0

v1 whole, which is shorter than its diff:
```python
import functools

import jax
import jax.numpy as jnp
import numpy as np
from jax import lax
from jax.experimental import pallas as pl
from jax.experimental.pallas import tpu as pltpu
from jax.sharding import PartitionSpec as P

STEPS = 4
CROPS_DEV = 12
SX, CZ, CY = 4, 16, 128
EZ, EY = 24, 256
HID = 64
VOX = 512

VELOCITY = (
    (0, 0, 0),
    (1, 0, 0),
    (-1, 0, 0),
    (0, 1, 0),
    (0, -1, 0),
    (0, 0, 1),
    (0, 0, -1),
    (1, 1, 0),
    (-1, -1, 0),
    (1, -1, 0),
    (-1, 1, 0),
    (1, 0, 1),
    (-1, 0, -1),
    (1, 0, -1),
    (-1, 0, 1),
    (0, 1, 1),
    (0, -1, -1),
    (0, 1, -1),
    (0, -1, 1),
)
WEIGHTS = (1.0 / 3.0,) + (1.0 / 18.0,) * 6 + (1.0 / 36.0,) * 12
OPPOSITE = (0, 2, 1, 4, 3, 6, 5, 8, 7, 10, 9, 12, 11, 14, 13, 16, 15, 18, 17)
OMEGA = 1.25
SCALE_DENSITY = 50.0
SCALE_FLOW = 30.0
F32 = jnp.float32
BF16 = jnp.bfloat16
MESH = pl.DeviceIdType.MESH


def signed_sum(entries, factors):
    running = None
    for entry, factor in zip(entries, factors):
        if factor == 0:
            continue
        if running is None:
            running = entry if factor > 0 else -entry
        else:
            running = running + entry if factor > 0 else running - entry
    return running


def moments(states):
    density = states[0]
    for number in range(1, 19):
        density = density + states[number]
    inverse = 1.0 / density
    flows = []
    for axis_id in range(3):
        summed = signed_sum(states, [VELOCITY[number][axis_id] for number in range(19)])
        flows.append(summed * inverse)
    return (density, flows[0], flows[1], flows[2])


def collide(states, wet_cells):
    density, flow_x, flow_y, flow_z = moments(states)
    flows = (flow_x, flow_y, flow_z)
    speed_sq = flow_x * flow_x + flow_y * flow_y + flow_z * flow_z
    base = 1.0 - 1.5 * speed_sq
    result = [None] * 19
    kept = 1.0 - OMEGA
    scaled = {w: (OMEGA * w) * density for w in set(WEIGHTS)}
    relaxed = kept * states[0] + scaled[WEIGHTS[0]] * base
    result[0] = jnp.where(wet_cells, relaxed, states[0])
    for number in range(1, 19, 2):
        other = OPPOSITE[number]
        along = signed_sum(flows, VELOCITY[number])
        weight = scaled[WEIGHTS[number]]
        even = weight * (base + (4.5 * along) * along)
        odd = weight * (3.0 * along)
        forth = kept * states[number] + (even + odd)
        back = kept * states[other] + (even - odd)
        result[number] = jnp.where(wet_cells, forth, states[other])
        result[other] = jnp.where(wet_cells, back, states[number])
    return result


def features(states, fluid):
    density, flow_x, flow_y, flow_z = moments(states)
    return [
        (density - 1.0) * SCALE_DENSITY * fluid,
        flow_x * SCALE_FLOW * fluid,
        flow_y * SCALE_FLOW * fluid,
        flow_z * SCALE_FLOW * fluid,
    ]


NT = (((1,), (1,)), ((), ()))
TN = (((0,), (0,)), ((), ()))


def dot(a, b, dims=(((1,), (0,)), ((), ()))):
    return lax.dot_general(a, b, dims, preferred_element_type=F32)


SHIFTS = [(a, b, c) for a in (-1, 0, 1) for b in (-1, 0, 1) for c in (-1, 0, 1)]


def lattice_kernel(
    ns,
    nn,
    pop_hbm,
    wall_hbm,
    w_lift,
    b_lift,
    w_mix,
    b_mix,
    w_head,
    b_head,
    anchors_hbm,
    spread_hbm,
    select_hbm,
    choose_hbm,
    inside_hbm,
    fin,
    patches,
    targets,
    wets,
    wall_w,
    wall,
    v_lift,
    v_blift,
    v_mix,
    v_bmix,
    v_head,
    v_bhead,
    anchors,
    spread,
    select,
    choose,
    inside,
    wb,
    small,
    early,
    late,
    windows,
    pack_l,
    pack_r,
    pack_u,
    pack_d,
    got_l,
    got_r,
    got_u,
    got_d,
    got_c,
    weights,
    cells,
    post,
    loads,
    halo_send,
    halo_recv,
    ag_send,
    ag_recv,
    fw_send,
    fw_recv,
):
    s = lax.axis_index("span")
    n = lax.axis_index("normal")
    chips = ns // 2
    chip = s // 2
    core = s % 2
    right, left = (s + 1) % ns, (s + ns - 1) % ns
    up, down = (n + 1) % nn, (n + nn - 1) % nn
    sibling = chip * 2 + (1 - core)

    def place(nn_, ss_):
        return {"normal": nn_, "span": ss_}

    fetches = [
        pltpu.make_async_copy(src, dst, loads.at[i])
        for i, (src, dst) in enumerate(
            (
                (pop_hbm, cells.at[0:19, :, 0:CZ, 0:CY]),
                (wall_hbm, wall),
                (w_lift, v_lift),
                (b_lift, v_blift),
                (w_mix, v_mix),
                (b_mix, v_bmix),
                (w_head, v_head),
                (b_head, v_bhead),
                (anchors_hbm, anchors),
                (spread_hbm, spread),
                (select_hbm, select),
                (choose_hbm, choose),
                (inside_hbm, inside),
            )
        )
    ]
    for copy in fetches:
        copy.start()

    peers = [
        place(n, right),
        place(n, left),
        place(up, s),
        place(down, s),
        place(up, right),
        place(up, left),
        place(down, right),
        place(down, left),
        place(n, sibling),
    ]
    z_peers = [((chip + k) % chips) * 2 + core for k in range(1, chips)]
    peers += [place(n, peer) for peer in z_peers]
    barrier = pltpu.get_barrier_semaphore()
    for peer in peers:
        pl.semaphore_signal(barrier, inc=1, device_id=peer, device_id_type=MESH)

    sub = lax.broadcasted_iota(jnp.int32, (8, 128), 0)
    low = sub < 4
    wb[...] = jnp.zeros((144, 128), F32)
    small[...] = jnp.zeros((16, 128), F32)
    fetches[0].wait()
    fetches[1].wait()
    cells[19, :, 0:CZ, 0:CY] = wall[...].astype(F32)

    for k in range(20):
        for j in range(2):
            t0, t1 = cells[k, 2 * j, 0:CZ, 0:CY], cells[k, 2 * j + 1, 0:CZ, 0:CY]
            pack_u[k, j] = jnp.where(low, pltpu.roll(t1[8:16], 4, 0), t0[8:16])
            pack_d[k, j] = jnp.where(low, t0[0:8], pltpu.roll(t1[0:8], 4, 0))
    slot = lax.broadcasted_iota(jnp.int32, (64, 128), 1) // 4
    pl_val = jnp.ones((64, 128), F32)
    pr_val = jnp.ones((64, 128), F32)
    for k in range(20):
        f = cells[k, :, 0:CZ, 0:CY].reshape(64, 128)
        rolled = pltpu.roll(f, 4 * k, 1) if k else f
        pl_val = jnp.where(slot == k, rolled, pl_val)
        pr_val = jnp.where(slot == (k - 1) % 32, rolled, pr_val)
    pack_l[...] = pl_val.reshape(SX, CZ, CY)
    pack_r[...] = pr_val.reshape(SX, CZ, CY)

    for copy in fetches[2:8]:
        copy.wait()
    wb[0:64, 0:108] = v_lift[0].astype(F32)
    wb[64:128, 0:64] = v_mix[0].astype(F32)
    small[0:1, 0:64] = v_blift[...].astype(F32)
    small[1:2, 0:64] = v_bmix[...].astype(F32)
    small[2:3, 0:4] = v_bhead[...].astype(F32)
    small[4:8, 0:64] = v_head[0].astype(F32)
    row16 = lax.broadcasted_iota(jnp.int32, (16, 128), 0)
    lane16 = lax.broadcasted_iota(jnp.int32, (16, 128), 1)
    head_at = (row16 >= 4) & (row16 < 8)
    head_at = head_at & ((lane16 == row16 + 108) | (lane16 == row16 + 112))
    to_top = ((row16 == 0) & (lane16 == 108)) | head_at
    to_mix = (row16 == 1) & (lane16 == 64)
    to_head = (row16 == 2) & (lane16 == 64)
    rows = small[...].astype(BF16)

    def turned(mask):
        return dot(rows, mask.astype(F32).astype(BF16), TN)

    seat = lax.broadcasted_iota(jnp.int32, (16, 128), 1)
    first = row16 % 12
    held = (row16 < 4) | (row16 >= 12)
    picks = (held & (seat == first)).astype(F32).astype(BF16)
    seat4 = lax.broadcasted_iota(jnp.int32, (16, 16), 1)
    row4 = lax.broadcasted_iota(jnp.int32, (16, 16), 0)
    picks4 = (((row4 < 4) | (row4 >= 12)) & (seat4 == row4 % 12 + 4)).astype(F32).astype(BF16)
    wb[0:64] = wb[0:64] + turned(to_top)[0:64]
    wb[64:128] = wb[64:128] + turned(to_mix)[0:64]
    wb[128:144] = dot(picks4, rows) + dot(picks, turned(to_head).astype(BF16))
    mine = wb[...].astype(BF16)
    weights[s] = mine
    wall_w[s] = mine

    pl.semaphore_wait(barrier, len(peers))

    def halo(i, src, dst, peer):
        return pltpu.make_async_remote_copy(
            src_ref=src,
            dst_ref=dst,
            send_sem=halo_send.at[i],
            recv_sem=halo_recv.at[i],
            device_id=peer,
            device_id_type=MESH,
        )

    top, bottom = pl.ds(8, 8), pl.ds(0, 8)
    sends = [
        halo(0, pack_u, got_u, place(up, s)),
        halo(1, pack_d, got_d, place(down, s)),
        halo(2, pack_l, got_l, place(n, left)),
        halo(3, pack_r, got_r, place(n, right)),
        halo(4, pack_l.at[:, bottom, :], got_c.at[0], place(down, left)),
        halo(5, pack_l.at[:, top, :], got_c.at[1], place(up, left)),
        halo(6, pack_r.at[:, bottom, :], got_c.at[2], place(down, right)),
        halo(7, pack_r.at[:, top, :], got_c.at[3], place(up, right)),
    ]
    for copy in sends:
        copy.start()

    gathers = []
    for k, peer in enumerate(z_peers):
        gathers.append(
            pltpu.make_async_remote_copy(
                src_ref=weights.at[s],
                dst_ref=weights.at[s],
                send_sem=ag_send.at[k],
                recv_sem=ag_recv.at[k],
                device_id=place(n, peer),
                device_id_type=MESH,
            )
        )
    for copy in gathers:
        copy.start()

    def forward(i, owner):
        return pltpu.make_async_remote_copy(
            src_ref=weights.at[owner],
            dst_ref=weights.at[owner],
            send_sem=fw_send.at[i],
            recv_sem=fw_recv.at[i],
            device_id=place(n, sibling),
            device_id_type=MESH,
        )

    forwards = [forward(0, s)]
    forwards[0].start()

    fluid = (1 - wall[...]).astype(F32)
    before = features([cells[q, :, 0:CZ, 0:CY] for q in range(19)], fluid)
    for c in range(4):
        early[:, c] = before[c].astype(BF16)
    early[:, 4] = fluid.astype(BF16)
    for copy in fetches[8:]:
        copy.wait()

    ahead = lax.broadcasted_iota(jnp.int32, (128, 256), 0)
    ahead = ahead - lax.broadcasted_iota(jnp.int32, (128, 256), 1) % 16
    unit_row = (lax.broadcasted_iota(jnp.int32, (40, VOX), 0) == 0).astype(F32)

    def cut(field, count, crop, window):
        ox = anchors[0, 0, crop, 0]
        near = field[ox].reshape(count * CZ, 128)
        far = field[(ox + 1) % SX].reshape(count * CZ, 128)
        wide = dot(jnp.concatenate([near, far], axis=0), window)
        return (wide * spread[0 : count * CZ * 2]).astype(BF16)

    def early_pair(i, carry):
        parts = []
        for j in range(2):
            crop = 2 * i + j
            oy = anchors[0, 0, crop, 1] % CY
            window = (ahead == oy).astype(F32).astype(BF16)
            windows[crop] = window
            parts.append(cut(early, 5, crop, window))
        got = dot(select[...], jnp.concatenate(parts, axis=0))
        x8 = jnp.concatenate([got[0:8], got[8:16]], axis=1)
        wets[i] = jnp.concatenate([got[16:24], got[24:32]], axis=1)
        moved = []
        for dx, dz, dy in SHIFTS:
            shift = (-(dx * 256 + dz * 16 + dy)) % VOX
            moved.append(pltpu.roll(x8, shift, 1) if shift else x8)
        moved.append(unit_row)
        patches[i] = jnp.concatenate(moved, axis=0).astype(BF16) * inside[...]
        return carry

    lax.fori_loop(0, CROPS_DEV // 2, early_pair, 0)

    for copy in sends:
        copy.wait()

    low4 = jnp.broadcast_to(low[None], (SX, 8, 128))
    edge_l = jnp.concatenate([got_l[...], jnp.where(low4, got_c[0], got_c[1])], axis=1)
    edge_r = jnp.concatenate([got_r[...], jnp.where(low4, got_c[2], got_c[3])], axis=1)
    edge_l = edge_l.reshape(SX * EZ, 128)
    edge_r = edge_r.reshape(SX * EZ, 128)
    odd = (lax.broadcasted_iota(jnp.int32, (SX * EZ, 128), 1) // 4) % 2 == 1
    mixed = (jnp.where(odd, edge_r, edge_l), jnp.where(odd, edge_l, edge_r))
    for k in range(20):
        side = mixed[k % 2]
        if k:
            side = pltpu.roll(side, 128 - 4 * k, 1)
        cells[k, :, :, CY:EY] = side.reshape(SX, EZ, 128)
        for j in range(2):
            u, d = got_u[k, j], got_d[k, j]
            cells[k, 2 * j, CZ:EZ, 0:CY] = jnp.where(low, d, u)
            cells[k, 2 * j + 1, CZ:EZ, 0:CY] = pltpu.roll(jnp.where(low, u, d), 4, 0)

    def one_step(step, carry):
        def one_chunk(i, inner):
            x = i // 3
            part = pl.ds(pl.multiple_of((i % 3) * 8, 8), 8)
            states = [cells[q, x, part, :] for q in range(19)]
            wet = cells[19, x, part, :] < 0.5
            for q, value in enumerate(collide(states, wet)):
                post[q, x, part, :] = value
            return inner

        lax.fori_loop(0, 12, one_chunk, 0)

        def one_slab(x, inner):
            for q in range(19):
                cx, cy, cz = VELOCITY[q]
                slab = post[q, (x + SX - cx) % SX]
                if cz:
                    slab = pltpu.roll(slab, cz % EZ, 0)
                if cy:
                    slab = pltpu.roll(slab, cy % EY, 1)
                cells[q, x] = slab
            return inner

        lax.fori_loop(0, SX, one_slab, 0)
        return carry

    lax.fori_loop(0, 2, one_step, 0)
    for k in range(1, chips):
        gathers[k - 1].wait()
        owner = ((chip + chips - k) % chips) * 2 + core
        copy = forward(k, owner)
        copy.start()
        forwards.append(copy)
        wall_w[owner] = weights[owner]
    lax.fori_loop(2, STEPS, one_step, 0)

    final = [cells[q, :, 0:CZ, 0:CY] for q in range(19)]
    for q in range(19):
        fin[q] = final[q]
    after = features(final, fluid)
    for c in range(4):
        late[:, c] = (after[c] - before[c]).astype(BF16)

    def late_pair(i, carry):
        parts = [cut(late, 4, 2 * i + j, windows[2 * i + j]) for j in range(2)]
        got = dot(choose[...], jnp.concatenate(parts, axis=0))
        targets[i] = jnp.concatenate([got[0:8], got[8:16]], axis=1)
        return carry

    lax.fori_loop(0, CROPS_DEV // 2, late_pair, 0)
    for copy in forwards:
        copy.wait()
    for k in range(chips):
        owner = ((chip + chips - k) % chips) * 2 + (1 - core)
        wall_w[owner] = weights[owner]


def gelu_both(x):
    c1, c2 = 0.7978845608028654, 0.7978845608028654 * 0.044715
    sq = x * x
    half = 0.5 * jnp.tanh(x * (c1 + c2 * sq)) + 0.5
    value = x * half
    slope = half + value * (1.0 - half) * (2.0 * c1 + 6.0 * c2 * sq)
    return value, slope


def constants():
    row = np.arange(160)
    lane = np.arange(256)
    spread = (lane[None, :] // 16 == row[:, None] % 16).astype(np.float32)
    select = np.zeros((32, 320), np.float32)
    choose = np.zeros((16, 256), np.float32)
    for xi in range(2):
        for i in range(8):
            crop, channel = i // 4, i % 4
            start = crop * 160 + xi * 80 + channel * 16
            select[xi * 8 + i, start : start + 16] = 1.0
            start = crop * 160 + xi * 80 + 64
            select[16 + xi * 8 + i, start : start + 16] = 1.0
            start = crop * 128 + xi * 64 + channel * 16
            choose[xi * 8 + i, start : start + 16] = 1.0
    expand = np.zeros((2, 128, 256), np.float32)
    for pos in range(2):
        for k in range(27):
            for c in range(4):
                expand[pos, 4 * k + c, 8 * k + 4 * pos + c] = 1.0
        expand[pos, 108, 216] = 1.0
    voxel = np.arange(VOX)
    vx, vz, vy = voxel // 256, voxel // 16 % 16, voxel % 16
    inside = np.ones((256, VOX), np.float32)
    for k, (dx, dz, dy) in enumerate(SHIFTS):
        good = (
            (vx + dx >= 0)
            & (vx + dx < 2)
            & (vz + dz >= 0)
            & (vz + dz < 16)
            & (vy + dy >= 0)
            & (vy + dy < 16)
        )
        inside[8 * k : 8 * k + 8] = good[None]
    return (
        (
            jnp.asarray(spread),
            jnp.asarray(select, BF16),
            jnp.asarray(choose, BF16),
            jnp.asarray(inside, BF16),
        ),
        (
            jnp.asarray(expand, BF16),
            jnp.asarray(np.transpose(expand, (0, 2, 1)), BF16),
        ),
    )


def train_kernel(
    ns,
    nn,
    trainers,
    patches_ref,
    targets,
    wets,
    wall_w,
    expand,
    shrink,
    out,
    crops,
    index,
    grads,
    pair,
    held,
    parts,
    zparts,
    mine,
    whole,
    pair_send,
    pair_recv,
    rs_send,
    rs_recv,
    z_send,
    z_recv,
    ag_send,
    ag_recv,
):
    s = lax.axis_index("span")
    n = lax.axis_index("normal")
    chips = ns // 2
    chip = s // 2
    core = s % 2
    sibling = chip * 2 + (1 - core)
    rows = 128 // nn
    n_peers = [(n + k) % nn for k in range(1, nn)]
    z_peers = [(chip + k) % chips for k in range(1, chips)]
    barrier = pltpu.get_barrier_semaphore()

    def at_span(other):
        return {"span": other, "normal": n}

    def at_normal(other):
        return {"span": s, "normal": other}

    peers = [at_span(sibling)]
    peers += [at_normal(other) for other in n_peers]
    peers += [at_span(other * 2 + core) for other in z_peers]
    for peer in peers:
        pl.semaphore_signal(barrier, inc=1, device_id=peer, device_id_type=MESH)

    def remember(m, carry):
        last, before = jnp.int32(CROPS_DEV), jnp.int32(CROPS_DEV)
        for c in range(CROPS_DEV):
            match = trainers[0, 0, c, 0] == m
            before = jnp.where(match, last, before)
            last = jnp.where(match, c, last)
        index[m, 0] = last
        index[m, 1] = before
        return carry

    lax.fori_loop(0, ns, remember, 0)
    crops[CROPS_DEV] = jnp.zeros((128, 128), F32)
    unit = (lax.broadcasted_iota(jnp.int32, (64, VOX), 0) == 0).astype(F32).astype(BF16)
    lane64 = lax.broadcasted_iota(jnp.int32, (64, 128), 1)
    lane128 = lax.broadcasted_iota(jnp.int32, (128, 128), 1)

    def one_pair(i, carry):
        owners = [trainers[0, 0, 2 * i + j, 0] for j in range(2)]
        t8, w8 = targets[i], wets[i]
        patches = patches_ref[i]
        mats = [wall_w[owner] for owner in owners]
        lift = jnp.concatenate(
            [dot(mats[j][0:64], expand[j]) for j in range(2)], axis=0
        ).astype(BF16)
        h1f, slope1 = gelu_both(dot(lift, patches))
        h1 = h1f.astype(BF16)
        slopes2, h1s, h2s, pred = [], [], [], None
        for j in range(2):
            own = h1[64 * j : 64 * j + 64]
            ext = jnp.concatenate([own, unit], axis=0)
            z2 = dot(mats[j][64:128], ext)
            g2, slope2 = gelu_both(z2)
            h2 = (own.astype(F32) + g2).astype(BF16)
            ext2 = jnp.concatenate([h2, unit], axis=0)
            got = dot(mats[j][128:144], ext2)[8 * j : 8 * j + 8]
            pred = got if pred is None else pred + got
            slopes2.append(slope2)
            h1s.append(ext)
            h2s.append(ext2)
        missed = pred - t8
        weighted = w8 * missed
        loss8 = weighted * missed * (1.0 / (4.0 * VOX))
        dpred = weighted * (2.0 / (4.0 * VOX))
        errors = jnp.concatenate([dpred, loss8], axis=0).astype(BF16)
        errors = jnp.concatenate([jnp.zeros((112, VOX), BF16), errors], axis=0)
        dh1s, firsts = [], []
        for j in range(2):
            low = 112 + 4 * j
            keep = (lane64 >= low) & (lane64 < low + 4)
            head = jnp.where(keep, mats[j][0:64].astype(F32), 0.0).astype(BF16)
            dh2 = dot(head, errors)
            dz2 = (dh2 * slopes2[j]).astype(BF16)
            back = dot(mats[j][64:128, 0:64], dz2, TN)
            dh1s.append(dh2 + back)
            mixed = dot(dz2, h1s[j], NT)
            heads = dot(h2s[j], errors, NT)
            own = (lane128 // 4) % 2 == j
            firsts.append((mixed, jnp.where(own, heads, 0.0)))
        dz1 = (jnp.concatenate(dh1s, axis=0) * slope1).astype(BF16)
        lifted = dot(dz1, patches, NT).astype(BF16)
        for j in range(2):
            mixed, heads = firsts[j]
            less = dot(lifted[64 * j : 64 * j + 64], shrink[j])
            upper = (less + heads[0:64]).astype(BF16).astype(F32)
            lower = mixed + heads[64:128]
            lower = jnp.where(lane64 < 64, lower.astype(BF16).astype(F32), lower)
            crops[2 * i + j, 0:64] = upper
            crops[2 * i + j, 64:128] = lower
        return carry

    lax.fori_loop(0, CROPS_DEV // 2, one_pair, 0)

    def member(m):
        return crops[index[m, 0]] + crops[index[m, 1]]

    def theirs(z, carry):
        grads[z] = member(2 * z + 1 - core)
        return carry

    lax.fori_loop(0, chips, theirs, 0)
    pl.semaphore_wait(barrier, len(peers))

    def remote(src, dst, send, recv, peer):
        copy = pltpu.make_async_remote_copy(
            src_ref=src,
            dst_ref=dst,
            send_sem=send,
            recv_sem=recv,
            device_id=peer,
            device_id_type=MESH,
        )
        copy.start()
        return copy

    first = remote(grads, pair, pair_send.at[0], pair_recv.at[0], at_span(sibling))

    def ours(z, carry):
        held[z] = member(2 * z + core)
        return carry

    lax.fori_loop(0, chips, ours, 0)
    first.wait()
    for z in range(chips):
        held[z] = held[z] + pair[z]
    seconds = []
    for k, other in enumerate(n_peers):
        chunk = pl.ds(pl.multiple_of(other * rows, 8), rows)
        seconds.append(
            remote(
                held.at[:, chunk, :],
                parts.at[k],
                rs_send.at[k],
                rs_recv.at[k],
                at_normal(other),
            )
        )
    own = held[:, pl.ds(pl.multiple_of(n * rows, 8), rows), :]
    for k in range(nn - 1):
        seconds[k].wait()
        own = own + parts[k]
    mine[...] = own
    thirds = []
    for k, other in enumerate(z_peers):
        thirds.append(
            remote(
                mine.at[other],
                zparts.at[k],
                z_send.at[k],
                z_recv.at[k],
                at_span(other * 2 + core),
            )
        )
    total = mine[chip]
    for k in range(chips - 1):
        thirds[k].wait()
        total = total + zparts[k]
    whole[n] = total * (1.0 / (CROPS_DEV * nn))
    fourths = []
    for k, other in enumerate(n_peers):
        fourths.append(
            remote(
                whole.at[n], whole.at[n], ag_send.at[k], ag_recv.at[k], at_normal(other)
            )
        )
    for copy in fourths:
        copy.wait()
    out[...] = whole[...]


def unpack_kernel(fin, total, o_fin, o_lift, o_blift, o_mix, o_bmix, o_head, o_bhead, o_loss, sem):
    copy = pltpu.make_async_copy(fin, o_fin, sem)
    copy.start()
    whole = total[...]
    turned = whole.T
    o_lift[0] = whole[0:64, 0:108]
    o_mix[0] = whole[64:128, 0:64]
    o_blift[...] = turned[108:109, 0:64]
    o_bmix[...] = turned[64:65, 64:128]
    heads = turned[112:120, 0:64]
    o_head[0] = heads[0:4] + heads[4:8]
    line = whole[64:65]
    o_bhead[...] = line[:, 112:116] + line[:, 116:120]
    lane = lax.broadcasted_iota(jnp.int32, (1, 128), 1)
    o_loss[...] = jnp.sum(jnp.where(lane >= 120, line, 0.0), axis=1, keepdims=True)
    copy.wait()


def local(
    populations, wall_mask, crop_anchors, trainers, w_lift, b_lift, w_mix, b_mix, w_head, b_head
):
    ns, nn = lax.axis_size("span"), lax.axis_size("normal")
    chips = ns // 2
    pairs = CROPS_DEV // 2
    vmem = pl.BlockSpec(memory_space=pltpu.VMEM)
    smem = pl.BlockSpec(memory_space=pltpu.SMEM)
    hbm = pl.BlockSpec(memory_space=pltpu.HBM)
    dma = pltpu.SemaphoreType.DMA
    shape = jax.ShapeDtypeStruct
    cutting, weighing = constants()
    spread, select, choose, inside = cutting
    edge = pltpu.VMEM((SX, CZ, CY), F32)
    flat = pltpu.VMEM((20, 2, 8, 128), F32)
    final, patches, targets, wets, wall_w = pl.pallas_call(
        functools.partial(lattice_kernel, ns, nn),
        out_shape=(
            shape((19, SX, CZ, CY), F32),
            shape((pairs, 256, VOX), BF16),
            shape((pairs, 8, VOX), F32),
            shape((pairs, 8, VOX), F32),
            shape((ns, 144, 128), BF16),
        ),
        in_specs=[hbm] * 13,
        out_specs=(vmem,) * 5,
        scratch_shapes=[
            pltpu.VMEM((SX, CZ, CY), jnp.int32),
            pltpu.VMEM(w_lift.shape, BF16),
            pltpu.VMEM(b_lift.shape, BF16),
            pltpu.VMEM(w_mix.shape, BF16),
            pltpu.VMEM(b_mix.shape, BF16),
            pltpu.VMEM(w_head.shape, BF16),
            pltpu.VMEM(b_head.shape, BF16),
            pltpu.SMEM(crop_anchors.shape, jnp.int32),
            pltpu.VMEM(spread.shape, F32),
            pltpu.VMEM(select.shape, BF16),
            pltpu.VMEM(choose.shape, BF16),
            pltpu.VMEM(inside.shape, BF16),
            pltpu.VMEM((144, 128), F32),
            pltpu.VMEM((16, 128), F32),
            pltpu.VMEM((SX, 5, CZ, CY), BF16),
            pltpu.VMEM((SX, 4, CZ, CY), BF16),
            pltpu.VMEM((CROPS_DEV, 128, 256), BF16),
            edge,
            edge,
            flat,
            flat,
            edge,
            edge,
            flat,
            flat,
            pltpu.VMEM((4, SX, 8, 128), F32),
            pltpu.VMEM((ns, 144, 128), BF16),
            pltpu.VMEM((20, SX, EZ, EY), F32),
            pltpu.VMEM((19, SX, EZ, EY), F32),
            dma((13,)),
            dma((8,)),
            dma((8,)),
            dma((chips,)),
            dma((chips,)),
            dma((chips,)),
            dma((chips,)),
        ],
        compiler_params=pltpu.CompilerParams(
            collective_id=0, has_side_effects=True, vmem_limit_bytes=32 << 20
        ),
        name="lattice",
    )(
        populations,
        wall_mask,
        w_lift,
        b_lift,
        w_mix,
        b_mix,
        w_head,
        b_head,
        crop_anchors,
        spread,
        select,
        choose,
        inside,
    )

    rows = 128 // nn
    total = pl.pallas_call(
        functools.partial(train_kernel, ns, nn),
        out_shape=shape((nn, rows, 128), F32),
        in_specs=[smem] + [vmem] * 6,
        out_specs=vmem,
        scratch_shapes=[
            pltpu.VMEM((CROPS_DEV + 1, 128, 128), F32),
            pltpu.SMEM((ns, 2), jnp.int32),
            pltpu.VMEM((chips, 128, 128), F32),
            pltpu.VMEM((chips, 128, 128), F32),
            pltpu.VMEM((chips, 128, 128), F32),
            pltpu.VMEM((nn - 1, chips, rows, 128), F32),
            pltpu.VMEM((chips - 1, rows, 128), F32),
            pltpu.VMEM((chips, rows, 128), F32),
            pltpu.VMEM((nn, rows, 128), F32),
            dma((1,)),
            dma((1,)),
            dma((nn - 1,)),
            dma((nn - 1,)),
            dma((chips - 1,)),
            dma((chips - 1,)),
            dma((nn - 1,)),
            dma((nn - 1,)),
        ],
        compiler_params=pltpu.CompilerParams(
            collective_id=1, has_side_effects=True, vmem_limit_bytes=32 << 20
        ),
        name="train",
    )(trainers, patches, targets, wets, wall_w, *weighing)

    outs = pl.pallas_call(
        unpack_kernel,
        out_shape=(
            shape(populations.shape, F32),
            shape(w_lift.shape, F32),
            shape(b_lift.shape, F32),
            shape(w_mix.shape, F32),
            shape(b_mix.shape, F32),
            shape(w_head.shape, F32),
            shape(b_head.shape, F32),
            shape((1, 1), F32),
        ),
        in_specs=[pl.BlockSpec(memory_space=pl.ANY), vmem],
        out_specs=(hbm,) + (vmem,) * 7,
        scratch_shapes=[pltpu.SemaphoreType.DMA],
        name="unpack",
    )(final, total.reshape(128, 128))
    return outs[:7] + (outs[7].reshape(1),)


def solution(mesh):
    return jax.shard_map(
        local,
        mesh=mesh,
        in_specs=(
            P(None, None, "normal", "span"),
            P(None, "normal", "span"),
            P("normal", "span", None, None),
            P("normal", "span", None, None),
            P("span", None, None),
            P("span", None),
            P("span", None, None),
            P("span", None),
            P("span", None, None),
            P("span", None),
        ),
        out_specs=(
            P(None, None, "normal", "span"),
            P("span", None, None),
            P("span", None),
            P("span", None, None),
            P("span", None),
            P("span", None, None),
            P("span", None),
            P("span"),
        ),
        check_vma=False,
    )
```

time: 73.6 us -> 94.8 us (1.29)
  Pallas kernels: 61.6 us -> 79.5 us
  local copies, waits for them, and re-layouts: 10.1 us -> 14 us
    pallas_call x3, Pallas kernels: 61.6 us -> 79.5 us  [the longest x1 34.7 us: local(): pl.pallas_call(functools.partial(train_kernel, ns, nn), out_shape=shape((...]
    unnamed x33 -> x34, local copies, waits for them, and re-layouts: 6.21 us -> 14 us
    broadcast_in_dim x6 -> x0, local copies, waits for them, and re-layouts: 1.25 us -> none  [the longest x1 0.62 us: local(): total[None, 64:, :64]]
    slice x2 -> x0, local copies, waits for them, and re-layouts: 1.21 us -> none  [the longest x1 0.7 us: local(): total[None, 64:, 64]]
where the time goes in v1:
time: 94.8 us; the launch traced here: 94.2 us
  Pallas kernels  79.5 us (84%)
  local copies, waits for them, and re-layouts  14 us (15%)
    pallas_call x1, Pallas kernels, local(): pl.pallas_call(functools.partial(train_kernel, ns, nn), out_shape=shape((...  34.7 us
    pallas_call x1, Pallas kernels, local(): pl.pallas_call(functools.partial(lattice_kernel, ns, nn), out_shape=(shap...  23.4 us
    pallas_call x1, Pallas kernels, local(): pl.pallas_call(unpack_kernel, out_shape=(shape(populations.shape, F32), s...  21.4 us
    unnamed x34, local copies, waits for them, and re-layouts  14 us

profile of v1, /device:TPU:8, one launch (start us, length us, event | category | flops | bytes accessed | tf_op | source)
XLA Modules:
  0.0 94.2 jit_solution(6770057551699512462)
XLA Ops:
  0.6 0.8 copy.24.anchors_hbm
  1.4 0.7 copy.25.trainers
  2.1 0.0 copy-start.1
  2.1 1.1 %copy-done.1 = f32[19,4,16,128]{3,2,1,0:T(8,128)S(1)} copy-done((f32[19,4,16,128]{3,2,1,0:T(8,128)S(1)}, f32[19,4,16,128]{3,2,1,0:T(8,128)}, u32[]{:S(2)}) %copy-start.1) | copy-done | bytes 622616
  3.2 0.9 %copy-done.2 = bf16[256,512]{1,0:T(8,128)(2,1)S(1)} copy-done((bf16[256,512]{1,0:T(8,128)(2,1)S(1)}, bf16[256,512]{1,0:T(8,128)(2,1)}, u32[]{:S(2)}) %copy-start.2) | copy-done | bytes 262168
  4.2 0.9 copy-done.4
  5.1 0.8 copy-done.7
  5.8 0.7 copy-done.8
  6.6 0.7 copy-done.9
  7.3 0.7 copy-done.10
  8.0 0.7 copy-done.11
  8.7 0.7 copy-done.12
  9.4 0.7 copy-done.13
  10.1 0.7 copy-done.14
  10.7 0.7 copy-done.15
  11.4 23.4 %lattice.1 = (f32[19,4,16,128]{3,2,1,0:T(8,128)S(1)}, bf16[6,256,512]{2,1,0:T(8,128)(2,1)S(1)}, f32[6,8,512]{2,1,0:T(8,128)S(1)}, f32[6,8,512]{2,1,0:T(8,128)S(1)}, bf16[16,144,128]{2,1,0:T(8,128)(2,1)S(1)}) custom-call(f32[19,4,16,128]{3,2,1,0:T(8,128)S(1)} %copy-done.1, s32[4,16,128]{2,1,0:T(8,128)S(1)} %copy-done.7, bf16[1,64,108]{2,1,0:T(8,128)(2,1)S(1)} %copy-done.9, ...), custom_call_target="tpu_custom_call" | custom-call | tf_op jit(solution)/shard_map/lattice/pallas_call | solution.py:747
  34.8 0.0 copy-start
  34.8 0.8 copy-done
  35.6 0.9 copy-done.5
  36.5 0.9 copy-done.6
  37.4 34.7 %train.1 = f32[16,8,128]{2,1,0:T(8,128)S(1)} custom-call(s32[1,1,12,1]{3,2,1,0:T(8,128)S(1)} %copy.25.trainers, bf16[6,256,512]{2,1,0:T(8,128)(2,1)S(1)} %get-tuple-element.22.patches_ref, f32[6,8,512]{2,1,0:T(8,128)S(1)} %get-tuple-element.23.targets, f32[6,8,512]{2,1,0:T(8,128)S(1)} %get-tuple-element.24.wets, ...), custom_call_target="tpu_custom_call" | custom-call | tf_op jit(solution)/shard_map/train/pallas_call | solution.py:817
  72.1 0.0 copy-start.3
  72.1 0.6 copy-done.3
  72.7 21.4 %unpack.1 = (f32[19,4,16,128]{3,2,1,0:T(8,128)}, f32[1,64,108]{2,1,0:T(8,128)}, f32[1,64]{1,0:T(1,128)}, f32[1,64,64]{2,1,0:T(8,128)}, f32[1,64]{1,0:T(1,128)}, ...) custom-call(f32[19,4,16,128]{3,2,1,0:T(8,128)} %copy-done, f32[128,128]{1,0:T(8,128)} %bitcast.2), custom_call_target="tpu_custom_call" | custom-call | tf_op jit(solution)/shard_map/unpack/pallas_call | solution.py:847
  (13 shorter events, 0.0 us)
Async XLA Ops:
  2.1 1.1 %copy-start.1 = (f32[19,4,16,128]{3,2,1,0:T(8,128)S(1)}, f32[19,4,16,128]{3,2,1,0:T(8,128)}, u32[]{:S(2)}) copy-start(f32[19,4,16,128]{3,2,1,0:T(8,128)} %pop_hbm.1) | copy-start | bytes 1867780
  3.2 0.9 %copy-start.2 = (bf16[256,512]{1,0:T(8,128)(2,1)S(1)}, bf16[256,512]{1,0:T(8,128)(2,1)}, u32[]{:S(2)}) copy-start(bf16[256,512]{1,0:T(8,128)(2,1)} %constant.15.clone.inside_hbm) | copy-start | bytes 786436
  4.2 0.9 copy-start.4
  5.1 0.8 copy-start.7
  5.8 0.7 copy-start.8
  6.6 0.7 copy-start.9
  7.3 0.7 copy-start.10
  8.0 0.7 copy-start.11
  8.7 0.7 copy-start.12
  9.4 0.7 copy-start.13
  10.1 0.7 copy-start.14
  10.7 0.7 copy-start.15
  34.8 0.8 copy-start
  35.6 0.9 copy-start.5
  36.5 0.9 copy-start.6
  72.1 0.6 copy-start.3

commit v2 on v1

--- a/solution.py
+++ b/solution.py
@@ -114,7 +114,7 @@
 SHIFTS = [(a, b, c) for a in (-1, 0, 1) for b in (-1, 0, 1) for c in (-1, 0, 1)]
 
 
-def lattice_kernel(
+def lattice_part(
     ns,
     nn,
     pop_hbm,
@@ -130,11 +130,13 @@
     select_hbm,
     choose_hbm,
     inside_hbm,
+    more_fetches,
+    n_peers,
     fin,
+    fin_sem,
     patches,
     targets,
     wets,
-    wall_w,
     wall,
     v_lift,
     v_blift,
@@ -201,6 +203,7 @@
                 (select_hbm, select),
                 (choose_hbm, choose),
                 (inside_hbm, inside),
+                *more_fetches,
             )
         )
     ]
@@ -210,8 +213,6 @@
     peers = [
         place(n, right),
         place(n, left),
-        place(up, s),
-        place(down, s),
         place(up, right),
         place(up, left),
         place(down, right),
@@ -220,6 +221,7 @@
     ]
     z_peers = [((chip + k) % chips) * 2 + core for k in range(1, chips)]
     peers += [place(n, peer) for peer in z_peers]
+    peers += [place(other, s) for other in n_peers]
     barrier = pltpu.get_barrier_semaphore()
     for peer in peers:
         pl.semaphore_signal(barrier, inc=1, device_id=peer, device_id_type=MESH)
@@ -280,7 +282,6 @@
     wb[128:144] = dot(picks4, rows) + dot(picks, turned(to_head).astype(BF16))
     mine = wb[...].astype(BF16)
     weights[s] = mine
-    wall_w[s] = mine
 
     pl.semaphore_wait(barrier, len(peers))
 
@@ -349,7 +350,7 @@
     unit_row = (lax.broadcasted_iota(jnp.int32, (40, VOX), 0) == 0).astype(F32)
 
     def cut(field, count, crop, window):
-        ox = anchors[0, 0, crop, 0]
+        ox = anchors[0, 0, 0, crop]
         near = field[ox].reshape(count * CZ, 128)
         far = field[(ox + 1) % SX].reshape(count * CZ, 128)
         wide = dot(jnp.concatenate([near, far], axis=0), window)
@@ -359,7 +360,7 @@
         parts = []
         for j in range(2):
             crop = 2 * i + j
-            oy = anchors[0, 0, crop, 1] % CY
+            oy = anchors[0, 0, 1, crop] % CY
             window = (ahead == oy).astype(F32).astype(BF16)
             windows[crop] = window
             parts.append(cut(early, 5, crop, window))
@@ -429,12 +430,11 @@
         copy = forward(k, owner)
         copy.start()
         forwards.append(copy)
-        wall_w[owner] = weights[owner]
     lax.fori_loop(2, STEPS, one_step, 0)
 
+    store = pltpu.make_async_copy(cells.at[0:19, :, 0:CZ, 0:CY], fin, fin_sem)
+    store.start()
     final = [cells[q, :, 0:CZ, 0:CY] for q in range(19)]
-    for q in range(19):
-        fin[q] = final[q]
     after = features(final, fluid)
     for c in range(4):
         late[:, c] = (after[c] - before[c]).astype(BF16)
@@ -448,9 +448,7 @@
     lax.fori_loop(0, CROPS_DEV // 2, late_pair, 0)
     for copy in forwards:
         copy.wait()
-    for k in range(chips):
-        owner = ((chip + chips - k) % chips) * 2 + (1 - core)
-        wall_w[owner] = weights[owner]
+    return store
 
 
 def gelu_both(x):
@@ -510,7 +508,7 @@
     )
 
 
-def train_kernel(
+def train_part(
     ns,
     nn,
     trainers,
@@ -548,24 +546,17 @@
     rows = 128 // nn
     n_peers = [(n + k) % nn for k in range(1, nn)]
     z_peers = [(chip + k) % chips for k in range(1, chips)]
-    barrier = pltpu.get_barrier_semaphore()
 
     def at_span(other):
         return {"span": other, "normal": n}
 
     def at_normal(other):
         return {"span": s, "normal": other}
-
-    peers = [at_span(sibling)]
-    peers += [at_normal(other) for other in n_peers]
-    peers += [at_span(other * 2 + core) for other in z_peers]
-    for peer in peers:
-        pl.semaphore_signal(barrier, inc=1, device_id=peer, device_id_type=MESH)
 
     def remember(m, carry):
         last, before = jnp.int32(CROPS_DEV), jnp.int32(CROPS_DEV)
         for c in range(CROPS_DEV):
-            match = trainers[0, 0, c, 0] == m
+            match = trainers[0, 0, 0, c] == m
             before = jnp.where(match, last, before)
             last = jnp.where(match, c, last)
         index[m, 0] = last
@@ -579,7 +570,7 @@
     lane128 = lax.broadcasted_iota(jnp.int32, (128, 128), 1)
 
     def one_pair(i, carry):
-        owners = [trainers[0, 0, 2 * i + j, 0] for j in range(2)]
+        owners = [trainers[0, 0, 0, 2 * i + j] for j in range(2)]
         t8, w8 = targets[i], wets[i]
         patches = patches_ref[i]
         mats = [wall_w[owner] for owner in owners]
@@ -642,8 +633,6 @@
         return carry
 
     lax.fori_loop(0, chips, theirs, 0)
-    pl.semaphore_wait(barrier, len(peers))
-
     def remote(src, dst, send, recv, peer):
         copy = pltpu.make_async_remote_copy(
             src_ref=src,
@@ -711,9 +700,75 @@
     out[...] = whole[...]
 
 
-def unpack_kernel(fin, total, o_fin, o_lift, o_blift, o_mix, o_bmix, o_head, o_bhead, o_loss, sem):
-    copy = pltpu.make_async_copy(fin, o_fin, sem)
-    copy.start()
+def fused_kernel(ns, nn, *refs):
+    (
+        pop,
+        wall,
+        w_lift,
+        b_lift,
+        w_mix,
+        b_mix,
+        w_head,
+        b_head,
+        anchors,
+        trainers,
+        spread,
+        select,
+        choose,
+        inside,
+        expand,
+        shrink,
+        fin,
+        total,
+    ) = refs[:18]
+    fin_sem, v_trainers, v_expand, v_shrink, patches, targets, wets, weights = refs[18:26]
+    lattice_refs, train_refs = refs[26:61], refs[61:]
+    n = lax.axis_index("normal")
+    n_peers = [(n + k) % nn for k in range(1, nn)]
+    store = lattice_part(
+        ns,
+        nn,
+        pop,
+        wall,
+        w_lift,
+        b_lift,
+        w_mix,
+        b_mix,
+        w_head,
+        b_head,
+        anchors,
+        spread,
+        select,
+        choose,
+        inside,
+        ((trainers, v_trainers), (expand, v_expand), (shrink, v_shrink)),
+        n_peers,
+        fin,
+        fin_sem,
+        patches,
+        targets,
+        wets,
+        *lattice_refs[:26],
+        weights,
+        *lattice_refs[26:],
+    )
+    train_part(
+        ns,
+        nn,
+        v_trainers,
+        patches,
+        targets,
+        wets,
+        weights,
+        v_expand,
+        v_shrink,
+        total,
+        *train_refs,
+    )
+    store.wait()
+
+
+def unpack_kernel(total, o_lift, o_blift, o_mix, o_bmix, o_head, o_bhead, o_loss):
     whole = total[...]
     turned = whole.T
     o_lift[0] = whole[0:64, 0:108]
@@ -726,7 +781,6 @@
     o_bhead[...] = line[:, 112:116] + line[:, 116:120]
     lane = lax.broadcasted_iota(jnp.int32, (1, 128), 1)
     o_loss[...] = jnp.sum(jnp.where(lane >= 120, line, 0.0), axis=1, keepdims=True)
-    copy.wait()
 
 
 def local(
@@ -736,7 +790,6 @@
     chips = ns // 2
     pairs = CROPS_DEV // 2
     vmem = pl.BlockSpec(memory_space=pltpu.VMEM)
-    smem = pl.BlockSpec(memory_space=pltpu.SMEM)
     hbm = pl.BlockSpec(memory_space=pltpu.HBM)
     dma = pltpu.SemaphoreType.DMA
     shape = jax.ShapeDtypeStruct
@@ -744,18 +797,21 @@
     spread, select, choose, inside = cutting
     edge = pltpu.VMEM((SX, CZ, CY), F32)
     flat = pltpu.VMEM((20, 2, 8, 128), F32)
-    final, patches, targets, wets, wall_w = pl.pallas_call(
-        functools.partial(lattice_kernel, ns, nn),
-        out_shape=(
-            shape((19, SX, CZ, CY), F32),
-            shape((pairs, 256, VOX), BF16),
-            shape((pairs, 8, VOX), F32),
-            shape((pairs, 8, VOX), F32),
-            shape((ns, 144, 128), BF16),
-        ),
-        in_specs=[hbm] * 13,
-        out_specs=(vmem,) * 5,
+    rows = 128 // nn
+    final, total = pl.pallas_call(
+        functools.partial(fused_kernel, ns, nn),
+        out_shape=(shape((19, SX, CZ, CY), F32), shape((nn, rows, 128), F32)),
+        in_specs=[hbm] * 16,
+        out_specs=(hbm, vmem),
         scratch_shapes=[
+            dma,
+            pltpu.SMEM((1, 1, 1, CROPS_DEV), jnp.int32),
+            pltpu.VMEM((2, 128, 256), BF16),
+            pltpu.VMEM((2, 256, 128), BF16),
+            pltpu.VMEM((pairs, 256, VOX), BF16),
+            pltpu.VMEM((pairs, 8, VOX), F32),
+            pltpu.VMEM((pairs, 8, VOX), F32),
+            pltpu.VMEM((ns, 144, 128), BF16),
             pltpu.VMEM((SX, CZ, CY), jnp.int32),
             pltpu.VMEM(w_lift.shape, BF16),
             pltpu.VMEM(b_lift.shape, BF16),
@@ -763,7 +819,7 @@
             pltpu.VMEM(b_mix.shape, BF16),
             pltpu.VMEM(w_head.shape, BF16),
             pltpu.VMEM(b_head.shape, BF16),
-            pltpu.SMEM(crop_anchors.shape, jnp.int32),
+            pltpu.SMEM((1, 1, 3, CROPS_DEV), jnp.int32),
             pltpu.VMEM(spread.shape, F32),
             pltpu.VMEM(select.shape, BF16),
             pltpu.VMEM(choose.shape, BF16),
@@ -782,44 +838,15 @@
             flat,
             flat,
             pltpu.VMEM((4, SX, 8, 128), F32),
-            pltpu.VMEM((ns, 144, 128), BF16),
             pltpu.VMEM((20, SX, EZ, EY), F32),
             pltpu.VMEM((19, SX, EZ, EY), F32),
-            dma((13,)),
+            dma((16,)),
             dma((8,)),
             dma((8,)),
             dma((chips,)),
             dma((chips,)),
             dma((chips,)),
             dma((chips,)),
-        ],
-        compiler_params=pltpu.CompilerParams(
-            collective_id=0, has_side_effects=True, vmem_limit_bytes=32 << 20
-        ),
-        name="lattice",
-    )(
-        populations,
-        wall_mask,
-        w_lift,
-        b_lift,
-        w_mix,
-        b_mix,
-        w_head,
-        b_head,
-        crop_anchors,
-        spread,
-        select,
-        choose,
-        inside,
-    )
-
-    rows = 128 // nn
-    total = pl.pallas_call(
-        functools.partial(train_kernel, ns, nn),
-        out_shape=shape((nn, rows, 128), F32),
-        in_specs=[smem] + [vmem] * 6,
-        out_specs=vmem,
-        scratch_shapes=[
             pltpu.VMEM((CROPS_DEV + 1, 128, 128), F32),
             pltpu.SMEM((ns, 2), jnp.int32),
             pltpu.VMEM((chips, 128, 128), F32),
@@ -839,15 +866,29 @@
             dma((nn - 1,)),
         ],
         compiler_params=pltpu.CompilerParams(
-            collective_id=1, has_side_effects=True, vmem_limit_bytes=32 << 20
+            collective_id=0, has_side_effects=True, vmem_limit_bytes=60 << 20
         ),
-        name="train",
-    )(trainers, patches, targets, wets, wall_w, *weighing)
-
+        name="channel",
+    )(
+        populations,
+        wall_mask,
+        w_lift,
+        b_lift,
+        w_mix,
+        b_mix,
+        w_head,
+        b_head,
+        jnp.swapaxes(crop_anchors, 2, 3),
+        jnp.swapaxes(trainers, 2, 3),
+        spread,
+        select,
+        choose,
+        inside,
+        *weighing,
+    )
     outs = pl.pallas_call(
         unpack_kernel,
         out_shape=(
-            shape(populations.shape, F32),
             shape(w_lift.shape, F32),
             shape(b_lift.shape, F32),
             shape(w_mix.shape, F32),
@@ -856,12 +897,11 @@
             shape(b_head.shape, F32),
             shape((1, 1), F32),
         ),
-        in_specs=[pl.BlockSpec(memory_space=pl.ANY), vmem],
-        out_specs=(hbm,) + (vmem,) * 7,
-        scratch_shapes=[pltpu.SemaphoreType.DMA],
+        in_specs=[vmem],
+        out_specs=(vmem,) * 7,
         name="unpack",
-    )(final, total.reshape(128, 128))
-    return outs[:7] + (outs[7].reshape(1),)
+    )(total.reshape(128, 128))
+    return (final,) + outs[:6] + (outs[6].reshape(1),)
 
 
 def solution(mesh):

time: 94.8 us -> 63 us (0.66)
  Pallas kernels: 79.5 us -> 58.9 us
  local copies, waits for them, and re-layouts: 14 us -> 3.21 us
    pallas_call x3 -> x2, Pallas kernels: 79.5 us -> 58.9 us  [the longest x1 57.3 us: local(): pl.pallas_call(functools.partial(fused_kernel, ns, nn), out_shape=(shape(...]
    unnamed x34 -> x4, local copies, waits for them, and re-layouts: 14 us -> 3.21 us
where the time goes in v2:
time: 63 us; the launch traced here: 62.8 us
  Pallas kernels  58.9 us (93%)
  local copies, waits for them, and re-layouts  3.21 us (5%)
  between operations  0.65 us (1%)
    pallas_call x1, Pallas kernels, local(): pl.pallas_call(functools.partial(fused_kernel, ns, nn), out_shape=(shape(...  57.3 us
    unnamed x4, local copies, waits for them, and re-layouts  3.21 us
    pallas_call x1, Pallas kernels, local(): pl.pallas_call(unpack_kernel, out_shape=(shape(w_lift.shape, F32), shape(...  1.6 us

profile of v2, /device:TPU:8, one launch (start us, length us, event | category | flops | bytes accessed | tf_op | source)
XLA Modules:
  0.0 62.8 jit_solution(11173973756607133598)
XLA Ops:
  0.6 0.0 copy-start
  0.6 0.7 %copy-done = s32[1,1,12,3]{2,1,3,0:T(1,128)S(1)} copy-done((s32[1,1,12,3]{2,1,3,0:T(1,128)S(1)}, s32[1,1,12,3]{2,1,3,0:T(1,128)}, u32[]{:S(2)}) %copy-start) | copy-done | bytes 168
  1.3 0.6 copy.26
  1.9 57.3 %channel.1 = (f32[19,4,16,128]{3,2,1,0:T(8,128)}, f32[16,8,128]{2,1,0:T(8,128)}) custom-call(f32[19,4,16,128]{3,2,1,0:T(8,128)} %refs_0_.1, s32[4,16,128]{2,1,0:T(8,128)} %refs_1_.1, bf16[1,64,108]{2,1,0:T(8,128)(2,1)} %refs_2_.1, bf16[1,64]{1,0:T(2,128)(2,1)} %refs_3_.1, bf16[1,64,64]{2,1,0:T(8,128)(2,1)} %refs_4_.1, bf16[1,64]{1,0:T(2,128)(2,1)} %refs_5_.1, ...), custom_call_target="tpu_custom_call" | custom-call | tf_op jit(solution)/shard_map/channel/pallas_call | solution.py:801
  59.2 1.6 %unpack.1 = (f32[1,64,108]{2,1,0:T(8,128)}, f32[1,64]{1,0:T(1,128)}, f32[1,64,64]{2,1,0:T(8,128)}, f32[1,64]{1,0:T(1,128)}, f32[1,4,64]{2,1,0:T(4,128)}, /*index=5*/f32[1,4]{1,0:T(1,128)}, f32[1,1]{1,0:T(1,128)}) custom-call(f32[128,128]{1,0:T(8,128)} %bitcast.6), custom_call_target="tpu_custom_call" | custom-call | tf_op jit(solution)/shard_map/unpack/pallas_call | solution.py:889
  60.8 2.0 %copy.28 = f32[19,4,16,128]{3,2,1,0:T(8,128)} copy(f32[19,4,16,128]{3,2,1,0:T(8,128)} %get-tuple-element.34) | data formatting | bytes 1245184
Async XLA Ops:
  0.6 0.7 %copy-start = (s32[1,1,12,3]{2,1,3,0:T(1,128)S(1)}, s32[1,1,12,3]{2,1,3,0:T(1,128)}, u32[]{:S(2)}) copy-start(s32[1,1,12,3]{2,1,3,0:T(1,128)} %param.18) | copy-start | bytes 436

commit v3 on v2

--- a/solution.py
+++ b/solution.py
@@ -10,6 +10,7 @@
 
 STEPS = 4
 CROPS_DEV = 12
+GROUP = 6
 SX, CZ, CY = 4, 16, 128
 EZ, EY = 24, 256
 HID = 64
@@ -132,6 +133,7 @@
     inside_hbm,
     more_fetches,
     n_peers,
+    meanwhile,
     fin,
     fin_sem,
     patches,
@@ -239,6 +241,24 @@
             t0, t1 = cells[k, 2 * j, 0:CZ, 0:CY], cells[k, 2 * j + 1, 0:CZ, 0:CY]
             pack_u[k, j] = jnp.where(low, pltpu.roll(t1[8:16], 4, 0), t0[8:16])
             pack_d[k, j] = jnp.where(low, t0[0:8], pltpu.roll(t1[0:8], 4, 0))
+    pl.semaphore_wait(barrier, len(peers))
+
+    def halo(i, src, dst, peer):
+        return pltpu.make_async_remote_copy(
+            src_ref=src,
+            dst_ref=dst,
+            send_sem=halo_send.at[i],
+            recv_sem=halo_recv.at[i],
+            device_id=peer,
+            device_id_type=MESH,
+        )
+
+    sends = [
+        halo(0, pack_u, got_u, place(up, s)),
+        halo(1, pack_d, got_d, place(down, s)),
+    ]
+    for copy in sends:
+        copy.start()
     slot = lax.broadcasted_iota(jnp.int32, (64, 128), 1) // 4
     pl_val = jnp.ones((64, 128), F32)
     pr_val = jnp.ones((64, 128), F32)
@@ -249,6 +269,19 @@
         pr_val = jnp.where(slot == (k - 1) % 32, rolled, pr_val)
     pack_l[...] = pl_val.reshape(SX, CZ, CY)
     pack_r[...] = pr_val.reshape(SX, CZ, CY)
+
+    top, bottom = pl.ds(8, 8), pl.ds(0, 8)
+    more = [
+        halo(2, pack_l, got_l, place(n, left)),
+        halo(3, pack_r, got_r, place(n, right)),
+        halo(4, pack_l.at[:, bottom, :], got_c.at[0], place(down, left)),
+        halo(5, pack_l.at[:, top, :], got_c.at[1], place(up, left)),
+        halo(6, pack_r.at[:, bottom, :], got_c.at[2], place(down, right)),
+        halo(7, pack_r.at[:, top, :], got_c.at[3], place(up, right)),
+    ]
+    for copy in more:
+        copy.start()
+    sends += more
 
     for copy in fetches[2:8]:
         copy.wait()
@@ -283,32 +316,6 @@
     mine = wb[...].astype(BF16)
     weights[s] = mine
 
-    pl.semaphore_wait(barrier, len(peers))
-
-    def halo(i, src, dst, peer):
-        return pltpu.make_async_remote_copy(
-            src_ref=src,
-            dst_ref=dst,
-            send_sem=halo_send.at[i],
-            recv_sem=halo_recv.at[i],
-            device_id=peer,
-            device_id_type=MESH,
-        )
-
-    top, bottom = pl.ds(8, 8), pl.ds(0, 8)
-    sends = [
-        halo(0, pack_u, got_u, place(up, s)),
-        halo(1, pack_d, got_d, place(down, s)),
-        halo(2, pack_l, got_l, place(n, left)),
-        halo(3, pack_r, got_r, place(n, right)),
-        halo(4, pack_l.at[:, bottom, :], got_c.at[0], place(down, left)),
-        halo(5, pack_l.at[:, top, :], got_c.at[1], place(up, left)),
-        halo(6, pack_r.at[:, bottom, :], got_c.at[2], place(down, right)),
-        halo(7, pack_r.at[:, top, :], got_c.at[3], place(up, right)),
-    ]
-    for copy in sends:
-        copy.start()
-
     gathers = []
     for k, peer in enumerate(z_peers):
         gathers.append(
@@ -360,7 +367,7 @@
         parts = []
         for j in range(2):
             crop = 2 * i + j
-            oy = anchors[0, 0, 1, crop] % CY
+            oy = anchors[0, 1, 0, crop] % CY
             window = (ahead == oy).astype(F32).astype(BF16)
             windows[crop] = window
             parts.append(cut(early, 5, crop, window))
@@ -377,6 +384,7 @@
 
     lax.fori_loop(0, CROPS_DEV // 2, early_pair, 0)
 
+    meanwhile()
     for copy in sends:
         copy.wait()
 
@@ -524,6 +532,7 @@
     grads,
     pair,
     held,
+    sent,
     parts,
     zparts,
     mine,
@@ -544,8 +553,8 @@
     core = s % 2
     sibling = chip * 2 + (1 - core)
     rows = 128 // nn
-    n_peers = [(n + k) % nn for k in range(1, nn)]
-    z_peers = [(chip + k) % chips for k in range(1, chips)]
+    n_peers = normal_peers(n, nn)
+    z_peers = [(chip + k) % chips for k in far_first(chips)]
 
     def at_span(other):
         return {"span": other, "normal": n}
@@ -553,86 +562,82 @@
     def at_normal(other):
         return {"span": s, "normal": other}
 
-    def remember(m, carry):
-        last, before = jnp.int32(CROPS_DEV), jnp.int32(CROPS_DEV)
-        for c in range(CROPS_DEV):
-            match = trainers[0, 0, 0, c] == m
-            before = jnp.where(match, last, before)
-            last = jnp.where(match, c, last)
-        index[m, 0] = last
-        index[m, 1] = before
-        return carry
-
-    lax.fori_loop(0, ns, remember, 0)
     crops[CROPS_DEV] = jnp.zeros((128, 128), F32)
     unit = (lax.broadcasted_iota(jnp.int32, (64, VOX), 0) == 0).astype(F32).astype(BF16)
     lane64 = lax.broadcasted_iota(jnp.int32, (64, 128), 1)
     lane128 = lax.broadcasted_iota(jnp.int32, (128, 128), 1)
 
-    def one_pair(i, carry):
-        owners = [trainers[0, 0, 0, 2 * i + j] for j in range(2)]
-        t8, w8 = targets[i], wets[i]
-        patches = patches_ref[i]
-        mats = [wall_w[owner] for owner in owners]
-        lift = jnp.concatenate(
-            [dot(mats[j][0:64], expand[j]) for j in range(2)], axis=0
-        ).astype(BF16)
-        h1f, slope1 = gelu_both(dot(lift, patches))
-        h1 = h1f.astype(BF16)
-        slopes2, h1s, h2s, pred = [], [], [], None
-        for j in range(2):
-            own = h1[64 * j : 64 * j + 64]
-            ext = jnp.concatenate([own, unit], axis=0)
-            z2 = dot(mats[j][64:128], ext)
-            g2, slope2 = gelu_both(z2)
-            h2 = (own.astype(F32) + g2).astype(BF16)
-            ext2 = jnp.concatenate([h2, unit], axis=0)
-            got = dot(mats[j][128:144], ext2)[8 * j : 8 * j + 8]
-            pred = got if pred is None else pred + got
-            slopes2.append(slope2)
-            h1s.append(ext)
-            h2s.append(ext2)
-        missed = pred - t8
-        weighted = w8 * missed
-        loss8 = weighted * missed * (1.0 / (4.0 * VOX))
-        dpred = weighted * (2.0 / (4.0 * VOX))
-        errors = jnp.concatenate([dpred, loss8], axis=0).astype(BF16)
-        errors = jnp.concatenate([jnp.zeros((112, VOX), BF16), errors], axis=0)
-        dh1s, firsts = [], []
-        for j in range(2):
-            low = 112 + 4 * j
-            keep = (lane64 >= low) & (lane64 < low + 4)
-            head = jnp.where(keep, mats[j][0:64].astype(F32), 0.0).astype(BF16)
-            dh2 = dot(head, errors)
-            dz2 = (dh2 * slopes2[j]).astype(BF16)
-            back = dot(mats[j][64:128, 0:64], dz2, TN)
-            dh1s.append(dh2 + back)
-            mixed = dot(dz2, h1s[j], NT)
-            heads = dot(h2s[j], errors, NT)
-            own = (lane128 // 4) % 2 == j
-            firsts.append((mixed, jnp.where(own, heads, 0.0)))
-        dz1 = (jnp.concatenate(dh1s, axis=0) * slope1).astype(BF16)
-        lifted = dot(dz1, patches, NT).astype(BF16)
-        for j in range(2):
-            mixed, heads = firsts[j]
-            less = dot(lifted[64 * j : 64 * j + 64], shrink[j])
-            upper = (less + heads[0:64]).astype(BF16).astype(F32)
-            lower = mixed + heads[64:128]
-            lower = jnp.where(lane64 < 64, lower.astype(BF16).astype(F32), lower)
-            crops[2 * i + j, 0:64] = upper
-            crops[2 * i + j, 64:128] = lower
+    def one_group(g, carry):
+        wide = range(GROUP)
+        both = range(2)
+        pairs = [g * GROUP + p for p in wide]
+        mats = [[wall_w[trainers[0, 0, 0, 2 * i + j]] for j in both] for i in pairs]
+        patches = [patches_ref[i] for i in pairs]
+        lift = [[dot(mats[p][j][0:64], expand[j]) for j in both] for p in wide]
+        lift = [jnp.concatenate(lift[p], axis=0).astype(BF16) for p in wide]
+        z1 = [dot(lift[p], patches[p]) for p in wide]
+        h1, slope1 = [], []
+        for p in wide:
+            value, slope = gelu_both(z1[p])
+            h1.append(value.astype(BF16))
+            slope1.append(slope)
+        own = [[h1[p][64 * j : 64 * j + 64] for j in both] for p in wide]
+        ext1 = [[jnp.concatenate([own[p][j], unit], axis=0) for j in both] for p in wide]
+        z2 = [[dot(mats[p][j][64:128], ext1[p][j]) for j in both] for p in wide]
+        ext2 = [[None, None] for p in wide]
+        slope2 = [[None, None] for p in wide]
+        for p in wide:
+            for j in both:
+                value, slope2[p][j] = gelu_both(z2[p][j])
+                h2 = (own[p][j].astype(F32) + value).astype(BF16)
+                ext2[p][j] = jnp.concatenate([h2, unit], axis=0)
+        pred = [
+            [dot(mats[p][j][128:144], ext2[p][j])[8 * j : 8 * j + 8] for j in both] for p in wide
+        ]
+        errors = []
+        for p in wide:
+            missed = pred[p][0] + pred[p][1] - targets[pairs[p]]
+            weighted = wets[pairs[p]] * missed
+            loss8 = weighted * missed * (1.0 / (4.0 * VOX))
+            dpred = weighted * (2.0 / (4.0 * VOX))
+            tail = jnp.concatenate([dpred, loss8], axis=0).astype(BF16)
+            errors.append(jnp.concatenate([jnp.zeros((112, VOX), BF16), tail], axis=0))
+        head = [
+            [jnp.where(keeps[j], mats[p][j][0:64].astype(F32), 0.0).astype(BF16) for j in both]
+            for p in wide
+        ]
+        dh2 = [[dot(head[p][j], errors[p]) for j in both] for p in wide]
+        dz2 = [[(dh2[p][j] * slope2[p][j]).astype(BF16) for j in both] for p in wide]
+        back = [[dot(mats[p][j][64:128, 0:64], dz2[p][j], TN) for j in both] for p in wide]
+        dh1 = [jnp.concatenate([dh2[p][j] + back[p][j] for j in both], axis=0) for p in wide]
+        dz1 = [(dh1[p] * slope1[p]).astype(BF16) for p in wide]
+        lifted = [dot(dz1[p], patches[p], NT).astype(BF16) for p in wide]
+        mixed = [[dot(dz2[p][j], ext1[p][j], NT) for j in both] for p in wide]
+        heads = [[dot(ext2[p][j], errors[p], NT) for j in both] for p in wide]
+        less = [[dot(lifted[p][64 * j : 64 * j + 64], shrink[j]) for j in both] for p in wide]
+        for p in wide:
+            for j in both:
+                mine_only = jnp.where(owned[j], heads[p][j], 0.0)
+                upper = (less[p][j] + mine_only[0:64]).astype(BF16).astype(F32)
+                lower = mixed[p][j] + mine_only[64:128]
+                lower = jnp.where(lane64 < 64, lower.astype(BF16).astype(F32), lower)
+                crops[2 * pairs[p] + j, 0:64] = upper
+                crops[2 * pairs[p] + j, 64:128] = lower
         return carry
 
-    lax.fori_loop(0, CROPS_DEV // 2, one_pair, 0)
+    keeps = [(lane64 >= 112 + 4 * j) & (lane64 < 116 + 4 * j) for j in range(2)]
+    owned = [(lane128 // 4) % 2 == j for j in range(2)]
+    lax.fori_loop(0, CROPS_DEV // 2 // GROUP, one_group, 0)
 
     def member(m):
         return crops[index[m, 0]] + crops[index[m, 1]]
 
     def theirs(z, carry):
-        grads[z] = member(2 * z + 1 - core)
+        grads[z] = member(2 * z + 1 - core).astype(BF16)
         return carry
 
     lax.fori_loop(0, chips, theirs, 0)
+
     def remote(src, dst, send, recv, peer):
         copy = pltpu.make_async_remote_copy(
             src_ref=src,
@@ -653,25 +658,20 @@
 
     lax.fori_loop(0, chips, ours, 0)
     first.wait()
-    for z in range(chips):
-        held[z] = held[z] + pair[z]
+    for z in range(0, chips, 2):
+        two = [held[z + i] + pair[z + i].astype(F32) for i in range(2)]
+        two = jnp.concatenate([v.reshape(nn, rows, 128) for v in two], axis=1)
+        sent[:, z * rows : (z + 2) * rows, :] = two.astype(BF16)
     seconds = []
     for k, other in enumerate(n_peers):
-        chunk = pl.ds(pl.multiple_of(other * rows, 8), rows)
         seconds.append(
-            remote(
-                held.at[:, chunk, :],
-                parts.at[k],
-                rs_send.at[k],
-                rs_recv.at[k],
-                at_normal(other),
-            )
+            remote(sent.at[other], parts.at[k], rs_send.at[k], rs_recv.at[k], at_normal(other))
         )
-    own = held[:, pl.ds(pl.multiple_of(n * rows, 8), rows), :]
+    own = sent[n].astype(F32)
     for k in range(nn - 1):
         seconds[k].wait()
-        own = own + parts[k]
-    mine[...] = own
+        own = own + parts[k].astype(F32)
+    mine[...] = own.reshape(chips, rows, 128)
     thirds = []
     for k, other in enumerate(z_peers):
         thirds.append(
@@ -700,6 +700,18 @@
     out[...] = whole[...]
 
 
+def far_first(count):
+    return sorted(range(1, count), key=lambda k: -min(k, count - k))
+
+
+def normal_peers(n, nn):
+    if nn != 16:
+        return [(n + k) % nn for k in range(1, nn)]
+    moves = [(i, j) for i in range(4) for j in range(4) if i or j]
+    moves.sort(key=lambda m: -(min(m[0], 4 - m[0]) + min(m[1], 4 - m[1])))
+    return [(n // 4 + i) % 4 * 4 + (n % 4 + j) % 4 for i, j in moves]
+
+
 def fused_kernel(ns, nn, *refs):
     (
         pop,
@@ -724,7 +736,20 @@
     fin_sem, v_trainers, v_expand, v_shrink, patches, targets, wets, weights = refs[18:26]
     lattice_refs, train_refs = refs[26:61], refs[61:]
     n = lax.axis_index("normal")
-    n_peers = [(n + k) % nn for k in range(1, nn)]
+    n_peers = normal_peers(n, nn)
+    def meanwhile():
+        def remember(m, carry):
+            last, before = jnp.int32(CROPS_DEV), jnp.int32(CROPS_DEV)
+            for c in range(CROPS_DEV):
+                match = v_trainers[0, 0, 0, c] == m
+                before = jnp.where(match, last, before)
+                last = jnp.where(match, c, last)
+            train_refs[1][m, 0] = last
+            train_refs[1][m, 1] = before
+            return carry
+
+        lax.fori_loop(0, ns, remember, 0)
+
     store = lattice_part(
         ns,
         nn,
@@ -743,6 +768,7 @@
         inside,
         ((trainers, v_trainers), (expand, v_expand), (shrink, v_shrink)),
         n_peers,
+        meanwhile,
         fin,
         fin_sem,
         patches,
@@ -768,8 +794,24 @@
     store.wait()
 
 
-def unpack_kernel(total, o_lift, o_blift, o_mix, o_bmix, o_head, o_bhead, o_loss):
-    whole = total[...]
+def unpack_kernel(
+    fin, total, o_fin, o_lift, o_blift, o_mix, o_bmix, o_head, o_bhead, o_loss, stage, whole_v, sems
+):
+    def hop(i, src, dst):
+        copy = pltpu.make_async_copy(src, dst, sems.at[i])
+        copy.start()
+        return copy
+
+    first = hop(8, total, whole_v)
+    edges = (0, 5, 10, 15, 19)
+    spans = [pl.ds(a, b - a) for a, b in zip(edges[:-1], edges[1:])]
+    reads = [hop(i, fin.at[span], stage.at[span]) for i, span in enumerate(spans)]
+    first.wait()
+    writes = []
+    for i, span in enumerate(spans):
+        reads[i].wait()
+        writes.append(hop(4 + i, stage.at[span], o_fin.at[span]))
+    whole = whole_v[...]
     turned = whole.T
     o_lift[0] = whole[0:64, 0:108]
     o_mix[0] = whole[64:128, 0:64]
@@ -781,6 +823,8 @@
     o_bhead[...] = line[:, 112:116] + line[:, 116:120]
     lane = lax.broadcasted_iota(jnp.int32, (1, 128), 1)
     o_loss[...] = jnp.sum(jnp.where(lane >= 120, line, 0.0), axis=1, keepdims=True)
+    for copy in writes:
+        copy.wait()
 
 
 def local(
@@ -819,7 +863,7 @@
             pltpu.VMEM(b_mix.shape, BF16),
             pltpu.VMEM(w_head.shape, BF16),
             pltpu.VMEM(b_head.shape, BF16),
-            pltpu.SMEM((1, 1, 3, CROPS_DEV), jnp.int32),
+            pltpu.SMEM((1, 3, 1, CROPS_DEV), jnp.int32),
             pltpu.VMEM(spread.shape, F32),
             pltpu.VMEM(select.shape, BF16),
             pltpu.VMEM(choose.shape, BF16),
@@ -849,10 +893,11 @@
             dma((chips,)),
             pltpu.VMEM((CROPS_DEV + 1, 128, 128), F32),
             pltpu.SMEM((ns, 2), jnp.int32),
+            pltpu.VMEM((chips, 128, 128), BF16),
+            pltpu.VMEM((chips, 128, 128), BF16),
             pltpu.VMEM((chips, 128, 128), F32),
-            pltpu.VMEM((chips, 128, 128), F32),
-            pltpu.VMEM((chips, 128, 128), F32),
-            pltpu.VMEM((nn - 1, chips, rows, 128), F32),
+            pltpu.VMEM((nn, chips * rows, 128), BF16),
+            pltpu.VMEM((nn - 1, chips * rows, 128), BF16),
             pltpu.VMEM((chips - 1, rows, 128), F32),
             pltpu.VMEM((chips, rows, 128), F32),
             pltpu.VMEM((nn, rows, 128), F32),
@@ -878,7 +923,7 @@
         b_mix,
         w_head,
         b_head,
-        jnp.swapaxes(crop_anchors, 2, 3),
+        jnp.transpose(crop_anchors, (0, 3, 1, 2)),
         jnp.swapaxes(trainers, 2, 3),
         spread,
         select,
@@ -889,6 +934,7 @@
     outs = pl.pallas_call(
         unpack_kernel,
         out_shape=(
+            shape(populations.shape, F32),
             shape(w_lift.shape, F32),
             shape(b_lift.shape, F32),
             shape(w_mix.shape, F32),
@@ -897,11 +943,17 @@
             shape(b_head.shape, F32),
             shape((1, 1), F32),
         ),
-        in_specs=[vmem],
-        out_specs=(vmem,) * 7,
+        in_specs=[hbm, hbm],
+        out_specs=(hbm,) + (vmem,) * 7,
+        scratch_shapes=[
+            pltpu.VMEM(populations.shape, F32),
+            pltpu.VMEM((128, 128), F32),
+            dma((9,)),
+        ],
+        compiler_params=pltpu.CompilerParams(vmem_limit_bytes=60 << 20),
         name="unpack",
-    )(total.reshape(128, 128))
-    return (final,) + outs[:6] + (outs[6].reshape(1),)
+    )(final, total.reshape(128, 128))
+    return outs[:7] + (outs[7].reshape(1),)
 
 
 def solution(mesh):

time: 63 us -> 50.8 us (0.81)
  Pallas kernels: 58.9 us -> 49.8 us
  local copies, waits for them, and re-layouts: 3.21 us -> 0 us
    pallas_call x1, Pallas kernels: 57.3 us -> 47.3 us  [local(): pl.pallas_call(functools.partial(fused_kernel, ns, nn), out_shape=(shape(...]
    unnamed x4 -> x0, local copies, waits for them, and re-layouts: 3.21 us -> none
    pallas_call x1, Pallas kernels: 1.6 us -> 2.56 us  [local(): pl.pallas_call(unpack_kernel, out_shape=(shape(populations.shape, F32), s...]
where the time goes in v3:
time: 50.8 us; the launch traced here: 50.5 us
  Pallas kernels  49.8 us (98%)
  between operations  0.64 us (1%)
    pallas_call x1, Pallas kernels, local(): pl.pallas_call(functools.partial(fused_kernel, ns, nn), out_shape=(shape(...  47.3 us
    pallas_call x1, Pallas kernels, local(): pl.pallas_call(unpack_kernel, out_shape=(shape(populations.shape, F32), s...  2.56 us

profile of v3, /device:TPU:8, one launch (start us, length us, event | category | flops | bytes accessed | tf_op | source)
XLA Modules:
  0.0 50.5 jit_solution(5018573353523906296)
XLA Ops:
  0.6 47.3 %channel.1 = (f32[19,4,16,128]{3,2,1,0:T(8,128)}, f32[16,8,128]{2,1,0:T(8,128)}) custom-call(f32[19,4,16,128]{3,2,1,0:T(8,128)} %refs_0_.1, s32[4,16,128]{2,1,0:T(8,128)} %refs_1_.1, bf16[1,64,108]{2,1,0:T(8,128)(2,1)} %refs_2_.1, bf16[1,64]{1,0:T(2,128)(2,1)} %refs_3_.1, bf16[1,64,64]{2,1,0:T(8,128)(2,1)} %refs_4_.1, bf16[1,64]{1,0:T(2,128)(2,1)} %refs_5_.1, ...), custom_call_target="tpu_custom_call" | custom-call | tf_op jit(solution)/shard_map/channel/pallas_call | solution.py:845
  47.9 2.6 %unpack.1 = (f32[19,4,16,128]{3,2,1,0:T(8,128)}, f32[1,64,108]{2,1,0:T(8,128)}, f32[1,64]{1,0:T(1,128)}, f32[1,64,64]{2,1,0:T(8,128)}, f32[1,64]{1,0:T(1,128)}, ...) custom-call(f32[19,4,16,128]{3,2,1,0:T(8,128)} %get-tuple-element.18.fin, f32[128,128]{1,0:T(8,128)} %bitcast.4), custom_call_target="tpu_custom_call" | custom-call | tf_op jit(solution)/shard_map/unpack/pallas_call | solution.py:934

commit v4 on v3

--- a/solution.py
+++ b/solution.py
@@ -209,24 +209,27 @@
             )
         )
     ]
-    for copy in fetches:
-        copy.start()
-
-    peers = [
-        place(n, right),
-        place(n, left),
+    fetches[0].start()
+    fetches[1].start()
+
+    z_peers = [((chip + k) % chips) * 2 + core for k in range(1, chips)]
+    far_z = [((chip + k) % chips) * 2 + core for k in far_first(chips)]
+    peers = [place(n, peer) for peer in far_z]
+    peers += [place(other, s) for other in n_peers]
+    peers += [
         place(up, right),
         place(up, left),
         place(down, right),
         place(down, left),
+        place(n, right),
+        place(n, left),
         place(n, sibling),
     ]
-    z_peers = [((chip + k) % chips) * 2 + core for k in range(1, chips)]
-    peers += [place(n, peer) for peer in z_peers]
-    peers += [place(other, s) for other in n_peers]
     barrier = pltpu.get_barrier_semaphore()
     for peer in peers:
         pl.semaphore_signal(barrier, inc=1, device_id=peer, device_id_type=MESH)
+    for copy in fetches[2:]:
+        copy.start()
 
     sub = lax.broadcasted_iota(jnp.int32, (8, 128), 0)
     low = sub < 4
@@ -236,9 +239,24 @@
     fetches[1].wait()
     cells[19, :, 0:CZ, 0:CY] = wall[...].astype(F32)
 
+    def own_chunk(i, inner):
+        x = i // 2
+        part = pl.ds(pl.multiple_of((i % 2) * 8, 8), 8)
+        states = [cells[q, x, part, 0:CY] for q in range(19)]
+        wet = cells[19, x, part, 0:CY] < 0.5
+        for q, value in enumerate(collide(states, wet)):
+            post[q, x, part, 0:CY] = value
+        return inner
+
+    lax.fori_loop(0, 8, own_chunk, 0, unroll=4)
+
+    def source(k):
+        return post.at[k] if k < 19 else cells.at[19]
+
     for k in range(20):
         for j in range(2):
-            t0, t1 = cells[k, 2 * j, 0:CZ, 0:CY], cells[k, 2 * j + 1, 0:CZ, 0:CY]
+            t0 = source(k)[2 * j, 0:CZ, 0:CY]
+            t1 = source(k)[2 * j + 1, 0:CZ, 0:CY]
             pack_u[k, j] = jnp.where(low, pltpu.roll(t1[8:16], 4, 0), t0[8:16])
             pack_d[k, j] = jnp.where(low, t0[0:8], pltpu.roll(t1[0:8], 4, 0))
     pl.semaphore_wait(barrier, len(peers))
@@ -263,7 +281,7 @@
     pl_val = jnp.ones((64, 128), F32)
     pr_val = jnp.ones((64, 128), F32)
     for k in range(20):
-        f = cells[k, :, 0:CZ, 0:CY].reshape(64, 128)
+        f = source(k)[:, 0:CZ, 0:CY].reshape(64, 128)
         rolled = pltpu.roll(f, 4 * k, 1) if k else f
         pl_val = jnp.where(slot == k, rolled, pl_val)
         pr_val = jnp.where(slot == (k - 1) % 32, rolled, pr_val)
@@ -385,7 +403,7 @@
     lax.fori_loop(0, CROPS_DEV // 2, early_pair, 0)
 
     meanwhile()
-    for copy in sends:
+    for copy in sends[2:]:
         copy.wait()
 
     low4 = jnp.broadcast_to(low[None], (SX, 8, 128))
@@ -399,11 +417,14 @@
         side = mixed[k % 2]
         if k:
             side = pltpu.roll(side, 128 - 4 * k, 1)
-        cells[k, :, :, CY:EY] = side.reshape(SX, EZ, 128)
+        source(k)[:, :, CY:EY] = side.reshape(SX, EZ, 128)
+    for copy in sends[:2]:
+        copy.wait()
+    for k in range(20):
         for j in range(2):
             u, d = got_u[k, j], got_d[k, j]
-            cells[k, 2 * j, CZ:EZ, 0:CY] = jnp.where(low, d, u)
-            cells[k, 2 * j + 1, CZ:EZ, 0:CY] = pltpu.roll(jnp.where(low, u, d), 4, 0)
+            source(k)[2 * j, CZ:EZ, 0:CY] = jnp.where(low, d, u)
+            source(k)[2 * j + 1, CZ:EZ, 0:CY] = pltpu.roll(jnp.where(low, u, d), 4, 0)
 
     def one_step(step, carry):
         def one_chunk(i, inner):
@@ -415,8 +436,11 @@
                 post[q, x, part, :] = value
             return inner
 
-        lax.fori_loop(0, 12, one_chunk, 0)
-
+        lax.fori_loop(0, 12, one_chunk, 0, unroll=6)
+        move()
+        return carry
+
+    def move():
         def one_slab(x, inner):
             for q in range(19):
                 cx, cy, cz = VELOCITY[q]
@@ -428,10 +452,10 @@
                 cells[q, x] = slab
             return inner
 
-        lax.fori_loop(0, SX, one_slab, 0)
-        return carry
-
-    lax.fori_loop(0, 2, one_step, 0)
+        lax.fori_loop(0, SX, one_slab, 0, unroll=4)
+
+    move()
+    one_step(1, 0)
     for k in range(1, chips):
         gathers[k - 1].wait()
         owner = ((chip + chips - k) % chips) * 2 + core
@@ -447,13 +471,10 @@
     for c in range(4):
         late[:, c] = (after[c] - before[c]).astype(BF16)
 
-    def late_pair(i, carry):
-        parts = [cut(late, 4, 2 * i + j, windows[2 * i + j]) for j in range(2)]
-        got = dot(choose[...], jnp.concatenate(parts, axis=0))
+    cuts = [cut(late, 4, crop, windows[crop]) for crop in range(CROPS_DEV)]
+    for i in range(CROPS_DEV // 2):
+        got = dot(choose[...], jnp.concatenate(cuts[2 * i : 2 * i + 2], axis=0))
         targets[i] = jnp.concatenate([got[0:8], got[8:16]], axis=1)
-        return carry
-
-    lax.fori_loop(0, CROPS_DEV // 2, late_pair, 0)
     for copy in forwards:
         copy.wait()
     return store
@@ -794,23 +815,20 @@
     store.wait()
 
 
-def unpack_kernel(
-    fin, total, o_fin, o_lift, o_blift, o_mix, o_bmix, o_head, o_bhead, o_loss, stage, whole_v, sems
-):
+def unpack_kernel(fin, total, *refs):
+    outs, stages, stage, whole_v, sems = refs[:8], refs[8:15], refs[15], refs[16], refs[17]
+    o_lift, o_blift, o_mix, o_bmix, o_head, o_bhead, o_loss = stages
+
     def hop(i, src, dst):
         copy = pltpu.make_async_copy(src, dst, sems.at[i])
         copy.start()
         return copy
 
-    first = hop(8, total, whole_v)
+    first = hop(0, total, whole_v)
     edges = (0, 5, 10, 15, 19)
     spans = [pl.ds(a, b - a) for a, b in zip(edges[:-1], edges[1:])]
-    reads = [hop(i, fin.at[span], stage.at[span]) for i, span in enumerate(spans)]
+    reads = [hop(1 + i, fin.at[span], stage.at[span]) for i, span in enumerate(spans)]
     first.wait()
-    writes = []
-    for i, span in enumerate(spans):
-        reads[i].wait()
-        writes.append(hop(4 + i, stage.at[span], o_fin.at[span]))
     whole = whole_v[...]
     turned = whole.T
     o_lift[0] = whole[0:64, 0:108]
@@ -823,6 +841,10 @@
     o_bhead[...] = line[:, 112:116] + line[:, 116:120]
     lane = lax.broadcasted_iota(jnp.int32, (1, 128), 1)
     o_loss[...] = jnp.sum(jnp.where(lane >= 120, line, 0.0), axis=1, keepdims=True)
+    writes = [hop(9 + i, stages[i], outs[1 + i]) for i in range(7)]
+    for i, span in enumerate(spans):
+        reads[i].wait()
+        writes.append(hop(5 + i, stage.at[span], outs[0].at[span]))
     for copy in writes:
         copy.wait()
 
@@ -931,29 +953,30 @@
         inside,
         *weighing,
     )
+    small = [
+        shape(w_lift.shape, F32),
+        shape(b_lift.shape, F32),
+        shape(w_mix.shape, F32),
+        shape(b_mix.shape, F32),
+        shape(w_head.shape, F32),
+        shape(b_head.shape, F32),
+        shape((1, 1), F32),
+    ]
     outs = pl.pallas_call(
         unpack_kernel,
-        out_shape=(
-            shape(populations.shape, F32),
-            shape(w_lift.shape, F32),
-            shape(b_lift.shape, F32),
-            shape(w_mix.shape, F32),
-            shape(b_mix.shape, F32),
-            shape(w_head.shape, F32),
-            shape(b_head.shape, F32),
-            shape((1, 1), F32),
-        ),
+        out_shape=[shape(populations.shape, F32)] + small,
         in_specs=[hbm, hbm],
-        out_specs=(hbm,) + (vmem,) * 7,
-        scratch_shapes=[
+        out_specs=[hbm] * 8,
+        scratch_shapes=[pltpu.VMEM(leaf.shape, F32) for leaf in small]
+        + [
             pltpu.VMEM(populations.shape, F32),
             pltpu.VMEM((128, 128), F32),
-            dma((9,)),
+            dma((16,)),
         ],
         compiler_params=pltpu.CompilerParams(vmem_limit_bytes=60 << 20),
         name="unpack",
     )(final, total.reshape(128, 128))
-    return outs[:7] + (outs[7].reshape(1),)
+    return tuple(outs[:7]) + (outs[7].reshape(1),)
 
 
 def solution(mesh):

time: 50.8 us -> 47.1 us (0.927)
  Pallas kernels: 49.8 us -> 46.3 us
    pallas_call x1, Pallas kernels: 47.3 us -> 44.3 us  [local(): pl.pallas_call(functools.partial(fused_kernel, ns, nn), out_shape=(shape(...]
    pallas_call x1, Pallas kernels: 2.56 us -> 1.98 us  [local(): pl.pallas_call(unpack_kernel, out_shape=[shape(populations.shape, F32)] +...]
where the time goes in v4:
time: 47.1 us; the launch traced here: 46.9 us
  Pallas kernels  46.3 us (98%)
  between operations  0.64 us (1%)
    pallas_call x1, Pallas kernels, local(): pl.pallas_call(functools.partial(fused_kernel, ns, nn), out_shape=(shape(...  44.3 us
    pallas_call x1, Pallas kernels, local(): pl.pallas_call(unpack_kernel, out_shape=[shape(populations.shape, F32)] +...  1.98 us

profile of v4, /device:TPU:8, one launch (start us, length us, event | category | flops | bytes accessed | tf_op | source)
XLA Modules:
  0.0 46.9 jit_solution(7789430551293624992)
XLA Ops:
  0.6 44.3 %channel.1 = (f32[19,4,16,128]{3,2,1,0:T(8,128)}, f32[16,8,128]{2,1,0:T(8,128)}) custom-call(f32[19,4,16,128]{3,2,1,0:T(8,128)} %refs_0_.1, s32[4,16,128]{2,1,0:T(8,128)} %refs_1_.1, bf16[1,64,108]{2,1,0:T(8,128)(2,1)} %refs_2_.1, bf16[1,64]{1,0:T(2,128)(2,1)} %refs_3_.1, bf16[1,64,64]{2,1,0:T(8,128)(2,1)} %refs_4_.1, bf16[1,64]{1,0:T(2,128)(2,1)} %refs_5_.1, ...), custom_call_target="tpu_custom_call" | custom-call | tf_op jit(solution)/shard_map/channel/pallas_call | solution.py:867
  44.9 2.0 %unpack.1 = (f32[19,4,16,128]{3,2,1,0:T(8,128)}, f32[1,64,108]{2,1,0:T(8,128)}, f32[1,64]{1,0:T(1,128)}, f32[1,64,64]{2,1,0:T(8,128)}, f32[1,64]{1,0:T(1,128)}, ...) custom-call(f32[19,4,16,128]{3,2,1,0:T(8,128)} %get-tuple-element.18.fin, f32[128,128]{1,0:T(8,128)} %bitcast.4), custom_call_target="tpu_custom_call" | custom-call | tf_op jit(solution)/shard_map/unpack/pallas_call | solution.py:965

commit v5 on v4

--- a/solution.py
+++ b/solution.py
@@ -456,13 +456,14 @@
 
     move()
     one_step(1, 0)
+    one_step(2, 0)
     for k in range(1, chips):
         gathers[k - 1].wait()
         owner = ((chip + chips - k) % chips) * 2 + core
         copy = forward(k, owner)
         copy.start()
         forwards.append(copy)
-    lax.fori_loop(2, STEPS, one_step, 0)
+    one_step(3, 0)
 
     store = pltpu.make_async_copy(cells.at[0:19, :, 0:CZ, 0:CY], fin, fin_sem)
     store.start()
@@ -657,7 +658,7 @@
         grads[z] = member(2 * z + 1 - core).astype(BF16)
         return carry
 
-    lax.fori_loop(0, chips, theirs, 0)
+    lax.fori_loop(0, chips, theirs, 0, unroll=chips)
 
     def remote(src, dst, send, recv, peer):
         copy = pltpu.make_async_remote_copy(
@@ -677,7 +678,7 @@
         held[z] = member(2 * z + core)
         return carry
 
-    lax.fori_loop(0, chips, ours, 0)
+    lax.fori_loop(0, chips, ours, 0, unroll=chips)
     first.wait()
     for z in range(0, chips, 2):
         two = [held[z + i] + pair[z + i].astype(F32) for i in range(2)]
@@ -816,7 +817,7 @@
 
 
 def unpack_kernel(fin, total, *refs):
-    outs, stages, stage, whole_v, sems = refs[:8], refs[8:15], refs[15], refs[16], refs[17]
+    outs, stages, sems = refs[:8], refs[8:15], refs[15]
     o_lift, o_blift, o_mix, o_bmix, o_head, o_bhead, o_loss = stages
 
     def hop(i, src, dst):
@@ -824,12 +825,8 @@
         copy.start()
         return copy
 
-    first = hop(0, total, whole_v)
-    edges = (0, 5, 10, 15, 19)
-    spans = [pl.ds(a, b - a) for a, b in zip(edges[:-1], edges[1:])]
-    reads = [hop(1 + i, fin.at[span], stage.at[span]) for i, span in enumerate(spans)]
-    first.wait()
-    whole = whole_v[...]
+    writes = [hop(0, fin, outs[0])]
+    whole = total[...].reshape(128, 128)
     turned = whole.T
     o_lift[0] = whole[0:64, 0:108]
     o_mix[0] = whole[64:128, 0:64]
@@ -841,10 +838,7 @@
     o_bhead[...] = line[:, 112:116] + line[:, 116:120]
     lane = lax.broadcasted_iota(jnp.int32, (1, 128), 1)
     o_loss[...] = jnp.sum(jnp.where(lane >= 120, line, 0.0), axis=1, keepdims=True)
-    writes = [hop(9 + i, stages[i], outs[1 + i]) for i in range(7)]
-    for i, span in enumerate(spans):
-        reads[i].wait()
-        writes.append(hop(5 + i, stage.at[span], outs[0].at[span]))
+    writes += [hop(1 + i, stages[i], outs[1 + i]) for i in range(7)]
     for copy in writes:
         copy.wait()
 
@@ -866,9 +860,9 @@
     rows = 128 // nn
     final, total = pl.pallas_call(
         functools.partial(fused_kernel, ns, nn),
-        out_shape=(shape((19, SX, CZ, CY), F32), shape((nn, rows, 128), F32)),
+        out_shape=(pltpu.VMEM((19, SX, CZ, CY), F32), pltpu.VMEM((nn, rows, 128), F32)),
         in_specs=[hbm] * 16,
-        out_specs=(hbm, vmem),
+        out_specs=(vmem, vmem),
         scratch_shapes=[
             dma,
             pltpu.SMEM((1, 1, 1, CROPS_DEV), jnp.int32),
@@ -965,17 +959,12 @@
     outs = pl.pallas_call(
         unpack_kernel,
         out_shape=[shape(populations.shape, F32)] + small,
-        in_specs=[hbm, hbm],
+        in_specs=[vmem, vmem],
         out_specs=[hbm] * 8,
-        scratch_shapes=[pltpu.VMEM(leaf.shape, F32) for leaf in small]
-        + [
-            pltpu.VMEM(populations.shape, F32),
-            pltpu.VMEM((128, 128), F32),
-            dma((16,)),
-        ],
-        compiler_params=pltpu.CompilerParams(vmem_limit_bytes=60 << 20),
+        scratch_shapes=[pltpu.VMEM(leaf.shape, F32) for leaf in small] + [dma((8,))],
+        compiler_params=pltpu.CompilerParams(vmem_limit_bytes=4 << 20),
         name="unpack",
-    )(final, total.reshape(128, 128))
+    )(final, total)
     return tuple(outs[:7]) + (outs[7].reshape(1),)
 
 

time: 47.1 us -> 45.1 us (0.958)
  Pallas kernels: 46.3 us -> 44.1 us
    pallas_call x1, Pallas kernels: 44.3 us -> 43.2 us  [local(): pl.pallas_call(functools.partial(fused_kernel, ns, nn), out_shape=(pltpu....]
    pallas_call x1, Pallas kernels: 1.98 us -> 0.92 us  [local(): pl.pallas_call(unpack_kernel, out_shape=[shape(populations.shape, F32)] +...]
where the time goes in v5:
time: 45.1 us; the launch traced here: 44.7 us
  Pallas kernels  44.1 us (98%)
  between operations  0.64 us (1%)
    pallas_call x1, Pallas kernels, local(): pl.pallas_call(functools.partial(fused_kernel, ns, nn), out_shape=(pltpu....  43.2 us
    pallas_call x1, Pallas kernels, local(): pl.pallas_call(unpack_kernel, out_shape=[shape(populations.shape, F32)] +...  0.92 us

profile of v5, /device:TPU:8, one launch (start us, length us, event | category | flops | bytes accessed | tf_op | source)
XLA Modules:
  0.0 44.7 jit_solution(8231193732087315521)
XLA Ops:
  0.6 43.2 %channel.1 = (f32[19,4,16,128]{3,2,1,0:T(8,128)S(1)}, f32[16,8,128]{2,1,0:T(8,128)S(1)}) custom-call(f32[19,4,16,128]{3,2,1,0:T(8,128)} %refs_0_.1, s32[4,16,128]{2,1,0:T(8,128)} %refs_1_.1, bf16[1,64,108]{2,1,0:T(8,128)(2,1)} %refs_2_.1, bf16[1,64]{1,0:T(2,128)(2,1)} %refs_3_.1, bf16[1,64,64]{2,1,0:T(8,128)(2,1)} %refs_4_.1, bf16[1,64]{1,0:T(2,128)(2,1)} %refs_5_.1, ...), custom_call_target="tpu_custom_call" | custom-call | tf_op jit(solution)/shard_map/channel/pallas_call | solution.py:861
  43.8 0.9 %unpack.1 = (f32[19,4,16,128]{3,2,1,0:T(8,128)}, f32[1,64,108]{2,1,0:T(8,128)}, f32[1,64]{1,0:T(1,128)}, f32[1,64,64]{2,1,0:T(8,128)}, f32[1,64]{1,0:T(1,128)}, ...) custom-call(f32[19,4,16,128]{3,2,1,0:T(8,128)S(1)} %get-tuple-element.18.fin, ...), custom_call_target="tpu_custom_call" | custom-call | tf_op jit(solution)/shard_map/unpack/pallas_call | solution.py:959

commit v6 on v5

--- a/solution.py
+++ b/solution.py
@@ -209,9 +209,6 @@
             )
         )
     ]
-    fetches[0].start()
-    fetches[1].start()
-
     z_peers = [((chip + k) % chips) * 2 + core for k in range(1, chips)]
     far_z = [((chip + k) % chips) * 2 + core for k in far_first(chips)]
     peers = [place(n, peer) for peer in far_z]
@@ -228,7 +225,7 @@
     barrier = pltpu.get_barrier_semaphore()
     for peer in peers:
         pl.semaphore_signal(barrier, inc=1, device_id=peer, device_id_type=MESH)
-    for copy in fetches[2:]:
+    for copy in fetches:
         copy.start()
 
     sub = lax.broadcasted_iota(jnp.int32, (8, 128), 0)
@@ -426,7 +423,7 @@
             source(k)[2 * j, CZ:EZ, 0:CY] = jnp.where(low, d, u)
             source(k)[2 * j + 1, CZ:EZ, 0:CY] = pltpu.roll(jnp.where(low, u, d), 4, 0)
 
-    def one_step(step, carry):
+    def one_step(step, carry, last=False):
         def one_chunk(i, inner):
             x = i // 3
             part = pl.ds(pl.multiple_of((i % 3) * 8, 8), 8)
@@ -437,10 +434,10 @@
             return inner
 
         lax.fori_loop(0, 12, one_chunk, 0, unroll=6)
-        move()
+        move(last)
         return carry
 
-    def move():
+    def move(last=False):
         def one_slab(x, inner):
             for q in range(19):
                 cx, cy, cz = VELOCITY[q]
@@ -449,7 +446,10 @@
                     slab = pltpu.roll(slab, cz % EZ, 0)
                 if cy:
                     slab = pltpu.roll(slab, cy % EY, 1)
-                cells[q, x] = slab
+                if last:
+                    fin[q, x] = slab[0:CZ, 0:CY]
+                else:
+                    cells[q, x] = slab
             return inner
 
         lax.fori_loop(0, SX, one_slab, 0, unroll=4)
@@ -463,11 +463,9 @@
         copy = forward(k, owner)
         copy.start()
         forwards.append(copy)
-    one_step(3, 0)
-
-    store = pltpu.make_async_copy(cells.at[0:19, :, 0:CZ, 0:CY], fin, fin_sem)
-    store.start()
-    final = [cells[q, :, 0:CZ, 0:CY] for q in range(19)]
+    one_step(3, 0, True)
+
+    final = [fin[q] for q in range(19)]
     after = features(final, fluid)
     for c in range(4):
         late[:, c] = (after[c] - before[c]).astype(BF16)
@@ -478,7 +476,6 @@
         targets[i] = jnp.concatenate([got[0:8], got[8:16]], axis=1)
     for copy in forwards:
         copy.wait()
-    return store
 
 
 def gelu_both(x):
@@ -772,7 +769,7 @@
 
         lax.fori_loop(0, ns, remember, 0)
 
-    store = lattice_part(
+    lattice_part(
         ns,
         nn,
         pop,
@@ -813,7 +810,6 @@
         total,
         *train_refs,
     )
-    store.wait()
 
 
 def unpack_kernel(fin, total, *refs):

time: 45.1 us -> 44.9 us (level)
  no operation moved by 1% of the time
where the time goes in v6:
time: 44.9 us; the launch traced here: 44.5 us
  Pallas kernels  43.8 us (98%)
  between operations  0.64 us (1%)
    pallas_call x1, Pallas kernels, local(): pl.pallas_call(functools.partial(fused_kernel, ns, nn), out_shape=(pltpu....  42.9 us
    pallas_call x1, Pallas kernels, local(): pl.pallas_call(unpack_kernel, out_shape=[shape(populations.shape, F32)] +...  0.92 us

profile of v6, /device:TPU:8, one launch (start us, length us, event | category | flops | bytes accessed | tf_op | source)
XLA Modules:
  0.0 44.5 jit_solution(2120760745492134311)
XLA Ops:
  0.6 42.9 %channel.1 = (f32[19,4,16,128]{3,2,1,0:T(8,128)S(1)}, f32[16,8,128]{2,1,0:T(8,128)S(1)}) custom-call(f32[19,4,16,128]{3,2,1,0:T(8,128)} %refs_0_.1, s32[4,16,128]{2,1,0:T(8,128)} %refs_1_.1, bf16[1,64,108]{2,1,0:T(8,128)(2,1)} %refs_2_.1, bf16[1,64]{1,0:T(2,128)(2,1)} %refs_3_.1, bf16[1,64,64]{2,1,0:T(8,128)(2,1)} %refs_4_.1, bf16[1,64]{1,0:T(2,128)(2,1)} %refs_5_.1, ...), custom_call_target="tpu_custom_call" | custom-call | tf_op jit(solution)/shard_map/channel/pallas_call | solution.py:857
  43.6 0.9 %unpack.1 = (f32[19,4,16,128]{3,2,1,0:T(8,128)}, f32[1,64,108]{2,1,0:T(8,128)}, f32[1,64]{1,0:T(1,128)}, f32[1,64,64]{2,1,0:T(8,128)}, f32[1,64]{1,0:T(1,128)}, ...) custom-call(f32[19,4,16,128]{3,2,1,0:T(8,128)S(1)} %get-tuple-element.18.fin, ...), custom_call_target="tpu_custom_call" | custom-call | tf_op jit(solution)/shard_map/unpack/pallas_call | solution.py:955

commit v7 on v6

--- a/solution.py
+++ b/solution.py
@@ -586,7 +586,36 @@
     lane64 = lax.broadcasted_iota(jnp.int32, (64, 128), 1)
     lane128 = lax.broadcasted_iota(jnp.int32, (128, 128), 1)
 
-    def one_group(g, carry):
+    def remote(src, dst, send, recv, peer):
+        copy = pltpu.make_async_remote_copy(
+            src_ref=src,
+            dst_ref=dst,
+            send_sem=send,
+            recv_sem=recv,
+            device_id=peer,
+            device_id_type=MESH,
+        )
+        copy.start()
+        return copy
+
+    def member(m):
+        return crops[index[m, 0]] + crops[index[m, 1]]
+
+    def send_half(half):
+        part = pl.ds(64 * half, 64)
+        for z in range(chips):
+            m = 2 * z + 1 - core
+            value = crops[index[m, 0], part] + crops[index[m, 1], part]
+            grads[half, z] = value.astype(BF16)
+        return remote(
+            grads.at[half],
+            pair.at[half],
+            pair_send.at[half],
+            pair_recv.at[half],
+            at_span(sibling),
+        )
+
+    def one_group(g):
         wide = range(GROUP)
         both = range(2)
         pairs = [g * GROUP + p for p in wide]
@@ -630,55 +659,39 @@
         back = [[dot(mats[p][j][64:128, 0:64], dz2[p][j], TN) for j in both] for p in wide]
         dh1 = [jnp.concatenate([dh2[p][j] + back[p][j] for j in both], axis=0) for p in wide]
         dz1 = [(dh1[p] * slope1[p]).astype(BF16) for p in wide]
-        lifted = [dot(dz1[p], patches[p], NT).astype(BF16) for p in wide]
         mixed = [[dot(dz2[p][j], ext1[p][j], NT) for j in both] for p in wide]
         heads = [[dot(ext2[p][j], errors[p], NT) for j in both] for p in wide]
+        for p in wide:
+            for j in both:
+                lower = mixed[p][j] + jnp.where(owned[j], heads[p][j], 0.0)[64:128]
+                lower = jnp.where(lane64 < 64, lower.astype(BF16).astype(F32), lower)
+                crops[2 * pairs[p] + j, 64:128] = lower
+        early = send_half(1)
+        lifted = [dot(dz1[p], patches[p], NT).astype(BF16) for p in wide]
         less = [[dot(lifted[p][64 * j : 64 * j + 64], shrink[j]) for j in both] for p in wide]
         for p in wide:
             for j in both:
                 mine_only = jnp.where(owned[j], heads[p][j], 0.0)
                 upper = (less[p][j] + mine_only[0:64]).astype(BF16).astype(F32)
-                lower = mixed[p][j] + mine_only[64:128]
-                lower = jnp.where(lane64 < 64, lower.astype(BF16).astype(F32), lower)
                 crops[2 * pairs[p] + j, 0:64] = upper
-                crops[2 * pairs[p] + j, 64:128] = lower
-        return carry
+        return early
 
     keeps = [(lane64 >= 112 + 4 * j) & (lane64 < 116 + 4 * j) for j in range(2)]
     owned = [(lane128 // 4) % 2 == j for j in range(2)]
-    lax.fori_loop(0, CROPS_DEV // 2 // GROUP, one_group, 0)
-
-    def member(m):
-        return crops[index[m, 0]] + crops[index[m, 1]]
-
-    def theirs(z, carry):
-        grads[z] = member(2 * z + 1 - core).astype(BF16)
-        return carry
-
-    lax.fori_loop(0, chips, theirs, 0, unroll=chips)
-
-    def remote(src, dst, send, recv, peer):
-        copy = pltpu.make_async_remote_copy(
-            src_ref=src,
-            dst_ref=dst,
-            send_sem=send,
-            recv_sem=recv,
-            device_id=peer,
-            device_id_type=MESH,
-        )
-        copy.start()
-        return copy
-
-    first = remote(grads, pair, pair_send.at[0], pair_recv.at[0], at_span(sibling))
+    early_half = one_group(0)
+
+    late_half = send_half(0)
 
     def ours(z, carry):
         held[z] = member(2 * z + core)
         return carry
 
     lax.fori_loop(0, chips, ours, 0, unroll=chips)
-    first.wait()
+    early_half.wait()
+    late_half.wait()
     for z in range(0, chips, 2):
-        two = [held[z + i] + pair[z + i].astype(F32) for i in range(2)]
+        got = [jnp.concatenate([pair[0, z + i], pair[1, z + i]], axis=0) for i in range(2)]
+        two = [held[z + i] + got[i].astype(F32) for i in range(2)]
         two = jnp.concatenate([v.reshape(nn, rows, 128) for v in two], axis=1)
         sent[:, z * rows : (z + 2) * rows, :] = two.astype(BF16)
     seconds = []
@@ -905,16 +918,16 @@
             dma((chips,)),
             pltpu.VMEM((CROPS_DEV + 1, 128, 128), F32),
             pltpu.SMEM((ns, 2), jnp.int32),
-            pltpu.VMEM((chips, 128, 128), BF16),
-            pltpu.VMEM((chips, 128, 128), BF16),
+            pltpu.VMEM((2, chips, 64, 128), BF16),
+            pltpu.VMEM((2, chips, 64, 128), BF16),
             pltpu.VMEM((chips, 128, 128), F32),
             pltpu.VMEM((nn, chips * rows, 128), BF16),
             pltpu.VMEM((nn - 1, chips * rows, 128), BF16),
             pltpu.VMEM((chips - 1, rows, 128), F32),
             pltpu.VMEM((chips, rows, 128), F32),
             pltpu.VMEM((nn, rows, 128), F32),
-            dma((1,)),
-            dma((1,)),
+            dma((2,)),
+            dma((2,)),
             dma((nn - 1,)),
             dma((nn - 1,)),
             dma((chips - 1,)),

time: 44.9 us -> 44.7 us (level)
  no operation moved by 1% of the time
where the time goes in v7:
time: 44.7 us; the launch traced here: 44.3 us
  Pallas kernels  43.6 us (98%)
  between operations  0.64 us (1%)
    pallas_call x1, Pallas kernels, local(): pl.pallas_call(functools.partial(fused_kernel, ns, nn), out_shape=(pltpu....  42.7 us
    pallas_call x1, Pallas kernels, local(): pl.pallas_call(unpack_kernel, out_shape=[shape(populations.shape, F32)] +...  0.92 us

profile of v7, /device:TPU:8, one launch (start us, length us, event | category | flops | bytes accessed | tf_op | source)
XLA Modules:
  0.0 44.3 jit_solution(11729118586775577438)
XLA Ops:
  0.6 42.7 %channel.1 = (f32[19,4,16,128]{3,2,1,0:T(8,128)S(1)}, f32[16,8,128]{2,1,0:T(8,128)S(1)}) custom-call(f32[19,4,16,128]{3,2,1,0:T(8,128)} %refs_0_.1, s32[4,16,128]{2,1,0:T(8,128)} %refs_1_.1, bf16[1,64,108]{2,1,0:T(8,128)(2,1)} %refs_2_.1, bf16[1,64]{1,0:T(2,128)(2,1)} %refs_3_.1, bf16[1,64,64]{2,1,0:T(8,128)(2,1)} %refs_4_.1, bf16[1,64]{1,0:T(2,128)(2,1)} %refs_5_.1, ...), custom_call_target="tpu_custom_call" | custom-call | tf_op jit(solution)/shard_map/channel/pallas_call | solution.py:870
  43.4 0.9 %unpack.1 = (f32[19,4,16,128]{3,2,1,0:T(8,128)}, f32[1,64,108]{2,1,0:T(8,128)}, f32[1,64]{1,0:T(1,128)}, f32[1,64,64]{2,1,0:T(8,128)}, f32[1,64]{1,0:T(1,128)}, ...) custom-call(f32[19,4,16,128]{3,2,1,0:T(8,128)S(1)} %get-tuple-element.18.fin, ...), custom_call_target="tpu_custom_call" | custom-call | tf_op jit(solution)/shard_map/unpack/pallas_call | solution.py:968
